TPU v7x, 256 devices: a whole 4x4x8 slice. The times are simulated.
256 devices in a mesh: src: 16 (over z, core), tgt: 16 (over y, x).
Axes of the slice: x: 4, y: 4, z: 8, core: 2. Of those that a mesh axis runs over, the one named last changes fastest.
Arguments:
- source_latent: float32 [32768, 32], P(('src', 'tgt')), may hold values from -1.5 to 1.5
- source_left: float32 [32768, 34], P(('src', 'tgt')), may hold values from -1 to 1
- source_right: float32 [32768, 34], P(('src', 'tgt')), may hold values from 0.1 to 1.9
- source_logw: float32 [32768], P(('src', 'tgt')), as said below
- target_latent: float32 [16, 16, 128, 32], P('tgt', 'src'), may hold values from -1.5 to 1.5
- target_left: float32 [16, 16, 128, 34], P('tgt', 'src'), may hold values from -1 to 1
- target_right: float32 [16, 16, 128, 34], P('tgt', 'src'), may hold values from 0.1 to 1.9
- target_logw: float32 [16, 16, 128], P('tgt', 'src'), as said below
- target_potential: float32 [16, 16, 128], P('tgt', 'src'), may hold values from -0.6 to 36
- old_moment: float32 [34, 34], replicated, may hold values from 0.05 to 0.5
Outputs:
- source_potential: float32 [32768], P('src')
- new_potential: float32 [32768], P('tgt')
Inputs may be any that keep to these rules, and one draw needn't show every extreme that they name: `source_logw`: log weights of the source cells, exp of which sums to about one. `target_logw`: log weights of the target cells, exp of which sums to about one.
All inputs are finite; a program needn't handle non-finite values.
Results may differ from a plain program's by a relative error of at most 0.0003.
Values sent between devices are 32-bit elements; how exact they have to be, the bound alone decides.
No kernel may reach another device: no remote copies, remote signals or barrier semaphores. Data moves between devices by JAX's collectives and lax.ppermute only.
A program may use at most 64 MiB of HBM per device.

v0:
```python
import jax
import jax.numpy as jnp
from jax import lax
from jax.sharding import PartitionSpec as P

ITERS = 2


entropy_weight = 0.1
joining_weight = 0.5


def build_cost(u, v, a1, a2, moment, row_sq, col_sq):
    left = jnp.concatenate(
        [
            u * (-2.0 * (1.0 - joining_weight)),
            jnp.dot(a1, moment, precision=lax.Precision.HIGHEST, preferred_element_type=jnp.float32)
            * (-2.0 * joining_weight),
        ],
        axis=1,
    )
    right = jnp.concatenate([v, a2], axis=1)
    cross = lax.dot_general(
        left,
        right,
        (((1,), (1,)), ((), ())),
        precision=lax.Precision.HIGHEST,
        preferred_element_type=jnp.float32,
    )
    return cross + (1.0 - joining_weight) * (row_sq[:, None] + col_sq[None, :])


def row_lse(scores):
    top = lax.pmax(jnp.max(scores, axis=1), "tgt")
    total = lax.psum(jnp.sum(jnp.exp(scores - top[:, None]), axis=1), "tgt")
    return top + jnp.log(total)


def col_lse(scores):
    top = lax.pmax(jnp.max(scores, axis=0), "src")
    total = lax.psum(jnp.sum(jnp.exp(scores - top[None, :]), axis=0), "src")
    return top + jnp.log(total)


def shards(
    source_latent,
    source_left,
    source_right,
    source_logw,
    target_latent,
    target_left,
    target_right,
    target_logw,
    target_potential,
    old_moment,
):
    u, a1, b1, la = (
        lax.all_gather(source_latent, "tgt", axis=0, tiled=True),
        lax.all_gather(source_left, "tgt", axis=0, tiled=True),
        lax.all_gather(source_right, "tgt", axis=0, tiled=True),
        lax.all_gather(source_logw, "tgt", axis=0, tiled=True),
    )
    v, a2, b2, lb, g = (
        lax.all_gather(target_latent, "src", axis=1, tiled=True),
        lax.all_gather(target_left, "src", axis=1, tiled=True),
        lax.all_gather(target_right, "src", axis=1, tiled=True),
        lax.all_gather(target_logw, "src", axis=1, tiled=True),
        lax.all_gather(target_potential, "src", axis=1, tiled=True),
    )
    v = v.reshape(-1, v.shape[-1])
    a2 = a2.reshape(-1, a2.shape[-1])
    b2 = b2.reshape(-1, b2.shape[-1])
    lb = lb.reshape(-1)
    g = g.reshape(-1)
    row_sq = jnp.sum(u * u, axis=1)
    col_sq = jnp.sum(v * v, axis=1)
    old_cost = build_cost(u, v, a1, a2, old_moment, row_sq, col_sq)
    f = entropy_weight * la - entropy_weight * row_lse((g[None, :] - old_cost) / entropy_weight)
    plan = jnp.exp((f[:, None] + g[None, :] - old_cost) / entropy_weight)
    carried = jnp.dot(plan, b2, precision=lax.Precision.HIGHEST, preferred_element_type=jnp.float32)
    summed = lax.psum(carried, "tgt")
    term = lax.dot_general(
        b1,
        summed,
        (((0,), (0,)), ((), ())),
        precision=lax.Precision.HIGHEST,
        preferred_element_type=jnp.float32,
    )
    moment = lax.psum(term, "src")
    joined = build_cost(u, v, a1, a2, moment, row_sq, col_sq)
    for step_index in range(ITERS):
        g = entropy_weight * lb - entropy_weight * col_lse((f[:, None] - joined) / entropy_weight)
        f = entropy_weight * la - entropy_weight * row_lse((g[None, :] - joined) / entropy_weight)
    return (f, g)


def solution(mesh):
    return jax.shard_map(
        shards,
        mesh=mesh,
        in_specs=(
            P(("src", "tgt"), None),
            P(("src", "tgt"), None),
            P(("src", "tgt"), None),
            P(("src", "tgt")),
            P("tgt", "src", None, None),
            P("tgt", "src", None, None),
            P("tgt", "src", None, None),
            P("tgt", "src", None),
            P("tgt", "src", None),
            P(),
        ),
        out_specs=(P("src"), P("tgt")),
        check_vma=False,
    )
```

profile of v0, /device:TPU:2, one launch (start us, length us, event | category | flops | bytes accessed | tf_op | source)
XLA Modules:
  0.0 730.1 jit_solution(3170595345932875201)
XLA Ops:
  7.2 20.9 %all_gather.32 = f32[1,16,128,32]{2,3,0,1:T(8,128)S(1)} all-gather(f32[1,1,128,32]{2,3,0,1:T(8,128)} %bitcast.66), channel_id=1, replica_groups=mesh['src'=16,'tgt'=16] {'src'}, dimensions={1}, use_global_device_ids=true | all-gather | bytes 278528 | tf_op jit(solution)/shard_map/all_gather | solution.py:64
  28.4 24.0 %all_gather.30 = f32[2048,32]{0,1:T(8,128)S(1)} all-gather(f32[128,32]{0,1:T(8,128)} %param.10), channel_id=1, replica_groups=mesh['src'=16,'tgt'=16] {'tgt'}, dimensions={0}, use_global_device_ids=true | all-gather | bytes 278528 | tf_op jit(solution)/shard_map/all_gather | solution.py:58
  52.5 15.2 %all_gather.33 = f32[1,16,128,34]{2,0,3,1:T(1,128)S(1)} all-gather(f32[1,1,128,34]{2,0,3,1:T(1,128)} %bitcast.64), channel_id=1, replica_groups=mesh['src'=16,'tgt'=16] {'src'}, dimensions={1}, use_global_device_ids=true | all-gather | bytes 295936 | tf_op jit(solution)/shard_map/all_gather | solution.py:65
  67.8 16.1 %all_gather.29 = f32[1,16,128]{2,0,1:T(1,128)S(1)} all-gather(f32[1,1,128]{2,0,1:T(1,128)} %bitcast.67), channel_id=1, replica_groups=mesh['src'=16,'tgt'=16] {'src'}, dimensions={1}, use_global_device_ids=true | all-gather | bytes 8704 | tf_op jit(solution)/shard_map/all_gather | solution.py:68
  83.9 22.2 %all_gather.31 = f32[2048,34]{0,1:T(8,128)S(1)} all-gather(f32[128,34]{0,1:T(8,128)} %param.11), channel_id=1, replica_groups=mesh['src'=16,'tgt'=16] {'tgt'}, dimensions={0}, use_global_device_ids=true | all-gather | bytes 295936 | tf_op jit(solution)/shard_map/all_gather | solution.py:59
  106.7 18.6 %fusion.7 = (f32[2048]{0:T(1024)S(1)}, f32[2048,2048]{0,1:T(8,128)}) fusion(f32[2048]{0:T(1024)S(1)} %bitcast.57, f32[2048]{0:T(1024)S(1)} %get-tuple-element.3, f32[2048]{0:T(1024)S(1)} %bitcast.61, f32[2048,66]{0,1:T(8,128)S(1)} %constant_dynamic-update-slice_fusion, f32[2048,32]{0,1:T(8,128)S(1)} %get-tuple-element.2, ...), kind=kOutput, calls=%fused_computation.18 | convolution fusion | flops 3347187712 | bytes 17891328 | tf_op jit(solution)/shard_map/dot_general | solution.py:23
  125.3 38.0 %pmax.35 = f32[2048]{0:T(1024)S(1)} all-reduce(f32[2048]{0:T(1024)S(1)} %get-tuple-element.4), channel_id=1, replica_groups=mesh['src'=16,'tgt'=16] {'tgt'}, use_global_device_ids=true, to_apply=%region_3.0 | all-reduce | flops 2048 | bytes 16384 | tf_op jit(solution)/shard_map/pmax | solution.py:34
  173.2 38.6 %psum.49 = f32[2048]{0:T(1024)S(1)} all-reduce(f32[2048]{0:T(1024)S(1)} %exponential_reduce_fusion.4), channel_id=1, replica_groups=mesh['src'=16,'tgt'=16] {'tgt'}, use_global_device_ids=true, to_apply=%region_5.0 | all-reduce | flops 2048 | bytes 16384 | tf_op jit(solution)/shard_map/psum | solution.py:35
  211.8 17.3 %all-gather = f32[16,1,128]{2,1,0:T(1,128)S(1)} all-gather(f32[1,1,128]{2,1,0:T(1,128)S(1)} %bitcast.68), channel_id=1, replica_groups=mesh['src'=16,'tgt'=16] {'tgt'}, dimensions={0}, use_global_device_ids=true | all-gather | bytes 8704 | tf_op jit(solution)/shard_map/all_gather | solution.py:61
  229.2 15.1 %all_gather.34 = f32[1,16,128,34]{2,0,3,1:T(1,128)S(1)} all-gather(f32[1,1,128,34]{2,0,3,1:T(1,128)S(1)} %bitcast.65), channel_id=1, replica_groups=mesh['src'=16,'tgt'=16] {'src'}, dimensions={1}, use_global_device_ids=true | all-gather | bytes 295936 | tf_op jit(solution)/shard_map/all_gather | solution.py:66
  244.5 18.4 %fusion = f32[2048,34]{0,1:T(8,128)} fusion(f32[2048,34]{0,1:T(8,128)S(1)} %bitcast.51, f32[2048,2048]{0,1:T(8,128)} %get-tuple-element.5, f32[2048]{0:T(1024)S(1)} %multiply_subtract_fusion.4, f32[2048]{0:T(1024)S(1)} %bitcast.59, f32[2048]{0:T(1024)S(1)} %get-tuple-element.3, f32[2048]{0:T(1024)S(1)} %bitcast.63), kind=kOutput, calls=%fused_computation.8 | convolution fusion | flops 1736441856 | bytes 17367040 | tf_op jit(solution)/shard_map/dot_general | solution.py:80
  263.0 16.0 %all_gather.28 = f32[1,16,128]{2,0,1:T(1,128)S(1)} all-gather(f32[1,1,128]{2,0,1:T(1,128)S(1)} %bitcast.69), channel_id=1, replica_groups=mesh['src'=16,'tgt'=16] {'src'}, dimensions={1}, use_global_device_ids=true | all-gather | bytes 8704 | tf_op jit(solution)/shard_map/all_gather | solution.py:67
  278.9 23.9 %all_gather.35 = f32[2048,34]{0,1:T(8,128)S(1)} all-gather(f32[128,34]{0,1:T(8,128)S(1)} %copy-done.2), channel_id=1, replica_groups=mesh['src'=16,'tgt'=16] {'tgt'}, dimensions={0}, use_global_device_ids=true | all-gather | bytes 295936 | tf_op jit(solution)/shard_map/all_gather | solution.py:60
  302.9 51.6 %all-reduce.2.cloned.1.call-done = f32[2048,34]{0,1:T(8,128)} async-done(((f32[2048,34]{0,1:T(8,128)}), f32[2048,34]{0,1:T(8,128)}) %all-reduce.2.cloned.1.call-update) | async-done | bytes 278544 | tf_op jit(solution)/shard_map/psum | solution.py:81
  355.8 46.5 %psum.51 = f32[34,34]{0,1:T(8,128)S(1)} all-reduce(f32[34,34]{0,1:T(8,128)S(1)} %convolution_bitcast_fusion), channel_id=1, replica_groups=mesh['src'=16,'tgt'=16] {'src'}, use_global_device_ids=true, to_apply=%region_7.0 | all-reduce | flops 1156 | bytes 9248 | tf_op jit(solution)/shard_map/psum | solution.py:89
  402.7 19.0 %fusion.8 = (f32[2048]{0:T(1024)S(1)}, f32[2048,2048]{0,1:T(8,128)}) fusion(f32[2048]{0:T(1024)S(1)} %multiply_subtract_fusion.4, f32[2048]{0:T(1024)S(1)} %bitcast.60, f32[2048]{0:T(1024)S(1)} %get-tuple-element.3, f32[2048,66]{0,1:T(8,128)S(1)} %constant_dynamic-update-slice_fusion, f32[2048,32]{0,1:T(8,128)S(1)} %get-tuple-element.2, ...), kind=kOutput, calls=%fused_computation.19 | convolution fusion | flops 3347187712 | bytes 17891328 | tf_op jit(solution)/shard_map/dot_general | solution.py:23
  421.7 24.0 %pmax.36 = f32[2048]{0:T(1024)S(1)} all-reduce(f32[2048]{0:T(1024)S(1)} %get-tuple-element.6), channel_id=1, replica_groups=mesh['src'=16,'tgt'=16] {'src'}, use_global_device_ids=true, to_apply=%region_9.0 | all-reduce | flops 2048 | bytes 16384 | tf_op jit(solution)/shard_map/pmax | solution.py:40
  453.8 24.3 %psum.52 = f32[2048]{0:T(1024)S(1)} all-reduce(f32[2048]{0:T(1024)S(1)} %exponential_reduce_fusion.3), channel_id=1, replica_groups=mesh['src'=16,'tgt'=16] {'src'}, use_global_device_ids=true, to_apply=%region_11.0 | all-reduce | flops 2048 | bytes 16384 | tf_op jit(solution)/shard_map/psum | solution.py:41
  485.5 37.4 %pmax.37 = f32[2048]{0:T(1024)S(1)} all-reduce(f32[2048]{0:T(1024)S(1)} %fusion.9), channel_id=1, replica_groups=mesh['src'=16,'tgt'=16] {'tgt'}, use_global_device_ids=true, to_apply=%region_13.0 | all-reduce | flops 2048 | bytes 16384 | tf_op jit(solution)/shard_map/pmax | solution.py:34
  530.9 38.6 %psum.53 = f32[2048]{0:T(1024)S(1)} all-reduce(f32[2048]{0:T(1024)S(1)} %exponential_reduce_fusion.2), channel_id=1, replica_groups=mesh['src'=16,'tgt'=16] {'tgt'}, use_global_device_ids=true, to_apply=%region_15.0 | all-reduce | flops 2048 | bytes 16384 | tf_op jit(solution)/shard_map/psum | solution.py:35
  577.1 24.1 %pmax.38 = f32[2048]{0:T(1024)S(1)} all-reduce(f32[2048]{0:T(1024)S(1)} %fusion.10), channel_id=1, replica_groups=mesh['src'=16,'tgt'=16] {'src'}, use_global_device_ids=true, to_apply=%region_17.0 | all-reduce | flops 2048 | bytes 16384 | tf_op jit(solution)/shard_map/pmax | solution.py:40
  609.1 24.1 %psum.54 = f32[2048]{0:T(1024)S(1)} all-reduce(f32[2048]{0:T(1024)S(1)} %exponential_reduce_fusion.1), channel_id=1, replica_groups=mesh['src'=16,'tgt'=16] {'src'}, use_global_device_ids=true, to_apply=%region_19.0 | all-reduce | flops 2048 | bytes 16384 | tf_op jit(solution)/shard_map/psum | solution.py:41
  640.7 36.0 %pmax.39 = f32[2048]{0:T(1024)S(1)} all-reduce(f32[2048]{0:T(1024)S(1)} %fusion.11), channel_id=1, replica_groups=mesh['src'=16,'tgt'=16] {'tgt'}, use_global_device_ids=true, to_apply=%region_21.0 | all-reduce | flops 2048 | bytes 16384 | tf_op jit(solution)/shard_map/pmax | solution.py:34
  684.6 38.0 %psum.55 = f32[2048]{0:T(1024)S(1)} all-reduce(f32[2048]{0:T(1024)S(1)} %exponential_reduce_fusion), channel_id=1, replica_groups=mesh['src'=16,'tgt'=16] {'tgt'}, use_global_device_ids=true, to_apply=%region_23.0 | all-reduce | flops 2048 | bytes 16384 | tf_op jit(solution)/shard_map/psum | solution.py:35
  (43 shorter events, 67.8 us)
Async XLA Ops:
  7.2 99.0 %copy-start = (f32[34,34]{1,0:T(8,128)S(1)}, f32[34,34]{1,0:T(8,128)}, u32[]{:S(2)}) copy-start(f32[34,34]{1,0:T(8,128)} %param.19) | copy-start | bytes 13876
  7.2 347.3 %all-reduce.2.cloned.1.call-start = ((), (), s32[]{:S(2)}) async-start(), calls=%async_computation | async-start | bytes 655360 | tf_op jit(solution)/shard_map/psum | solution.py:81
  106.7 105.1 %copy-start.4 = (f32[128]{0:T(128)S(1)}, f32[128]{0:T(128)}, u32[]{:S(2)}) copy-start(f32[128]{0:T(128)} %param.13) | copy-start | bytes 1540
  106.7 122.5 %copy-start.3 = (f32[1,1,128,34]{2,1,3,0:T(1,128)S(1)}, f32[1,1,128,34]{2,1,3,0:T(1,128)}, u32[]{:S(2)}) copy-start(f32[1,1,128,34]{2,1,3,0:T(1,128)} %param.16) | copy-start | bytes 52228
  244.5 18.5 %copy-start.5 = (f32[1,1,128]{2,1,0:T(1,128)S(1)}, f32[1,1,128]{2,1,0:T(1,128)}, u32[]{:S(2)}) copy-start(f32[1,1,128]{2,1,0:T(1,128)} %param.17) | copy-start | bytes 1540
  244.5 34.4 %copy-start.2 = (f32[128,34]{0,1:T(8,128)S(1)}, f32[128,34]{0,1:T(8,128)}, u32[]{:S(2)}) copy-start(f32[128,34]{0,1:T(8,128)} %param.12) | copy-start | bytes 52228
  633.2 51.4 %copy-start.1 = (f32[2048]{0:T(1024)}, f32[2048]{0:T(1024)S(1)}, u32[]{:S(2)}) copy-start(f32[2048]{0:T(1024)S(1)} %multiply_subtract_fusion.1) | copy-start | bytes 24580
Sparse Core Ops, SparseCore 0:
  263.1 91.3 all-reduce.1
where the time goes:
time: 731 us; the launch traced here: 730 us
  blocking collectives  540 us (74%)
  other arithmetic  64.9 us (9%)
  matrix products  58.3 us (8%)
  waiting for transfers between devices  51.6 us (7%)
  between operations  14.4 us (2%)
    psum x3, blocking collectives, row_lse(): total = lax.psum(jnp.sum(jnp.exp(scores - top[:, None]), axis=1), 'tgt')  115 us
    pmax x3, blocking collectives, row_lse(): top = lax.pmax(jnp.max(scores, axis=1), 'tgt')  111 us
    psum x1, waiting for transfers between devices, shards(): summed = lax.psum(carried, 'tgt')  51.6 us
    psum x2, blocking collectives, col_lse(): total = lax.psum(jnp.sum(jnp.exp(scores - top[None, :]), axis=0), 'src')  48.3 us
    pmax x2, blocking collectives, col_lse(): top = lax.pmax(jnp.max(scores, axis=0), 'src')  48.1 us
    psum x1, blocking collectives, shards(): moment = lax.psum(term, 'src')  46.5 us
    dot_general x2, matrix products, build_cost(): lax.dot_general(left, right, (((1,), (1,)), ((), ())), precision=lax.Prec...  37.6 us
    reduce_sum x3, other arithmetic, row_lse(): total = lax.psum(jnp.sum(jnp.exp(scores - top[:, None]), axis=1), 'tgt')  25.8 us
  transfers between devices with their start and end apart: 1, of which 1 were waited for; matrix products, arithmetic and copies ran while one was open for 0% of the time, Pallas kernels for 0%

commit v1 on v0

v1 whole, which is shorter than its diff:
```python
import functools

import jax
import jax.numpy as jnp
from jax import lax
from jax.experimental import pallas as pl
from jax.experimental.pallas import tpu as pltpu
from jax.sharding import PartitionSpec as P

LATENT = 32
RANK = 34
FEAT = 80
BIAS = 3 * FEAT
DEPTH = 256
LANES = 128
ENTROPY = 0.1
LOG2E = 1.4426950408889634
SCALE = LOG2E / ENTROPY

ROW_LOGW = LATENT + RANK
ROW_POT = ROW_LOGW + 1
ROW_RIGHT = 72
PACK = 112

f32 = jnp.float32
bf16 = jnp.bfloat16


def dot(a, b):
    return jnp.dot(a, b, preferred_element_type=f32)


def dot_nt(a, b):
    return lax.dot_general(a, b, (((1,), (1,)), ((), ())), preferred_element_type=f32)


def split(x):
    hi = x.astype(bf16)
    return hi, (x - hi.astype(f32)).astype(bf16)


def iota(shape, axis):
    return lax.broadcasted_iota(jnp.int32, shape, axis)


def eye():
    shape = (LANES, LANES)
    return iota(shape, 0) == iota(shape, 1)


def to_lanes(column, mask):
    return jnp.sum(jnp.where(mask, column, 0.0), axis=0, keepdims=True)


def tile(t):
    return slice(t * LANES, (t + 1) * LANES)


def features(block):
    x = block[0:FEAT]
    return jnp.where(iota(x.shape, 0) < LATENT + RANK, x, 0.0)


def half_square(block):
    x = block[0:LATENT]
    return 0.5 * jnp.sum(x * x, axis=0, keepdims=True)


def put_bias(ref, potential):
    rows = iota((16, LANES), 0)
    for t in range(potential.shape[0]):
        x = potential[t : t + 1]
        hi = x.astype(bf16).astype(f32)
        rest = x - hi
        mid = rest.astype(bf16).astype(f32)
        low = rest - mid
        block = jnp.where(rows == 0, hi, jnp.where(rows == 1, mid, jnp.where(rows == 2, low, 0.0)))
        ref[BIAS:DEPTH, tile(t)] = block.astype(bf16)


def ones_block():
    shape = (DEPTH - BIAS, LANES)
    return jnp.where(iota(shape, 0) < 3, 1.0, 0.0).astype(bf16)


def left_operand(xh, xl, moment):
    shape = (LANES, LANES)
    row, column = iota(shape, 0), iota(shape, 1)
    mixed = moment.T + jnp.where((row == column) & (row < LATENT), 1.0, 0.0)
    qh, ql = split((SCALE * mixed)[0:FEAT, 0:FEAT])
    both = dot(jnp.concatenate([qh, ql], axis=0), xh)
    return split(both[0:FEAT] + both[FEAT:] + dot(qh, xl))


def transpose_into(ref, t, block):
    unit = jnp.where(eye(), 1.0, 0.0).astype(bf16)
    ref[tile(t), :] = dot_nt(unit, block).astype(bf16)


def lse_rows(stream, fixed, out_ref, n, blocks):
    mask = eye()

    def step(b, carry):
        rows = pl.ds(pl.multiple_of(b * LANES, LANES), LANES)
        s = dot(stream[rows, :], fixed[...])
        top = s[:, tile(0)]
        for t in range(1, blocks):
            top = jnp.maximum(top, s[:, tile(t)])
        total = jnp.exp2(s[:, tile(0)] - top)
        for t in range(1, blocks):
            total = total + jnp.exp2(s[:, tile(t)] - top)
        whole = jnp.max(top, axis=1, keepdims=True)
        total = jnp.sum(total * jnp.exp2(top - whole), axis=1, keepdims=True)
        lse = to_lanes(whole + jnp.log2(total), mask)
        for k in range(n):
            out_ref[k, pl.ds(b, 1), :] = lse
        return carry

    lax.fori_loop(0, stream.shape[0] // LANES, step, 0)


def combine(parts):
    top = jnp.max(parts, axis=0)
    return top + jnp.log2(jnp.sum(jnp.exp2(parts - top[None]), axis=0))


def old_kernel(n, blocks, sg, tg, moment, lse_out, lse_own, carried, xh, xl, rt, rc, lc, b2c):
    for t in range(blocks):
        hi, low = split(features(sg[t]))
        xh[:, tile(t)] = hi
        xl[:, tile(t)] = low
        hi, low = split(features(tg[t]))
        rt[0:FEAT, tile(t)] = hi
        rt[FEAT : 2 * FEAT, tile(t)] = low
        rt[2 * FEAT : BIAS, tile(t)] = hi
        transpose_into(rc, t, jnp.concatenate([hi, low, hi, ones_block()], axis=0))
        right = jnp.concatenate([tg[t, ROW_RIGHT:PACK, :], jnp.zeros((8, LANES), f32)], axis=0)
        right = jnp.where(iota(right.shape, 0) < RANK, right, 0.0)
        hi, low = split(right)
        block = jnp.concatenate([jnp.zeros((LATENT, LANES), bf16), hi, low], axis=0)
        b2c[tile(t), :] = dot_nt(jnp.where(eye(), 1.0, 0.0).astype(bf16), block).astype(bf16)
    lh, ll = left_operand(xh[...], xl[...], moment[...])
    for t in range(blocks):
        block = jnp.concatenate([lh[:, tile(t)], lh[:, tile(t)], ll[:, tile(t)], ones_block()], axis=0)
        transpose_into(lc, t, block)
    pot = [SCALE * (tg[t, ROW_POT : ROW_POT + 1, :] - half_square(tg[t])) for t in range(blocks)]
    put_bias(rt, jnp.concatenate(pot, axis=0))
    mask = eye()

    def step(b, carry):
        rows = pl.ds(pl.multiple_of(b * LANES, LANES), LANES)
        s = dot(lc[rows, :], rt[...])
        whole = jnp.max(s, axis=1, keepdims=True)
        p = jnp.exp2(s - whole)
        total = jnp.sum(p, axis=1, keepdims=True)
        hi, low = split(p)
        c = dot(hi, b2c[...]) + dot(low, b2c[...])
        carried[rows, :] = c / total
        lse = to_lanes(whole + jnp.log2(total), mask)
        for k in range(n):
            lse_out[k, pl.ds(b, 1), :] = lse
        lse_own[pl.ds(b, 1), :] = lse
        return carry

    lax.fori_loop(0, blocks, step, 0)


def moment_kernel(n, blocks, parts, lse_own, carried, sg, f_out, moment_out):
    logw = jnp.concatenate([sg[t, ROW_LOGW : ROW_LOGW + 1, :] for t in range(blocks)], axis=0)
    f = LOG2E * logw - combine(parts[...])
    f_out[...] = f
    weight = jnp.exp2(f + lse_own[...])
    hi, low = [], []
    for t in range(blocks):
        a, b = split(sg[t, ROW_RIGHT:PACK, :] * weight[t : t + 1])
        hi.append(a)
        low.append(b)
    hi, low = jnp.concatenate(hi, axis=1), jnp.concatenate(low, axis=1)
    ch, cl = split(carried[...])
    term = dot(hi, ch) + dot(low, ch) + dot(hi, cl)
    term = term + pltpu.roll(term, LANES - 48, 1)
    for k in range(n):
        moment_out[k] = term


def sum_kernel(n, parts, out):
    total = jnp.sum(parts[...], axis=0)
    for k in range(n):
        out[k] = total


def first_g_kernel(n, blocks, parts, f, xh, xl, rc, out, lc, lt):
    total = jnp.sum(parts[...], axis=0)
    rows, lanes = iota(total.shape, 0), iota(total.shape, 1)
    keep = (rows < RANK) & (lanes >= LATENT) & (lanes < LATENT + RANK)
    total = jnp.where(keep, total, 0.0)
    moment = jnp.concatenate([jnp.zeros((LATENT, LANES), f32), total, jnp.zeros((56, LANES), f32)], axis=0)
    lh, ll = left_operand(xh[...], xl[...], moment)
    lt[0:FEAT, :] = lh
    lt[FEAT : 2 * FEAT, :] = lh
    lt[2 * FEAT : BIAS, :] = ll
    for t in range(blocks):
        transpose_into(lc, t, jnp.concatenate([lt[0:BIAS, tile(t)], ones_block()], axis=0))
    put_bias(lt, f[...])
    lse_rows(rc, lt, out, n, blocks)


def half_kernel(n, blocks, parts, gathered, stream, fixed, out, pot_out, scratch):
    logw = jnp.concatenate([gathered[t, ROW_LOGW : ROW_LOGW + 1, :] for t in range(blocks)], axis=0)
    x = LOG2E * logw - combine(parts[...])
    square = jnp.concatenate([half_square(gathered[t]) for t in range(blocks)], axis=0)
    pot_out[...] = x * (1.0 / SCALE) + square
    scratch[0:BIAS, :] = fixed[0:BIAS, :]
    put_bias(scratch, x)
    lse_rows(stream, scratch, out, n, blocks)


def last_kernel(blocks, parts, gathered, pot_out):
    logw = jnp.concatenate([gathered[t, ROW_LOGW : ROW_LOGW + 1, :] for t in range(blocks)], axis=0)
    x = LOG2E * logw - combine(parts[...])
    square = jnp.concatenate([half_square(gathered[t]) for t in range(blocks)], axis=0)
    pot_out[...] = x * (1.0 / SCALE) + square


def call(kernel, out, scratch=(), name=None):
    spec = pl.BlockSpec(memory_space=pltpu.VMEM)
    return lambda *args: pl.pallas_call(
        kernel,
        out_shape=[jax.ShapeDtypeStruct(s, d) for s, d in out],
        in_specs=[spec] * len(args),
        out_specs=[spec] * len(out),
        scratch_shapes=[pltpu.VMEM(s, d) for s, d in scratch],
        compiler_params=pltpu.CompilerParams(vmem_limit_bytes=32 * 1024 * 1024),
        name=name,
    )(*args)


def pack(latent, left, right, logw, potential):
    cells = latent.shape[0]
    rows = [latent.T, left.T, logw[None], potential[None], jnp.zeros((ROW_RIGHT - ROW_POT - 1, cells), f32)]
    return jnp.concatenate(rows + [right.T, jnp.zeros((PACK - ROW_RIGHT - RANK, cells), f32)], axis=0)


def spread(x, n):
    return jnp.broadcast_to(x[None], (n,) + x.shape)


def swap(x, axis):
    return lax.all_to_all(x, axis, 0, 0)


def shards(n_src, n_tgt, *args):
    (u, a1, b1, la, v, a2, b2, lb, g, old_moment) = args
    v, a2, b2 = (x.reshape(-1, x.shape[-1]) for x in (v, a2, b2))
    lb, g = lb.reshape(-1), g.reshape(-1)
    sg = swap(spread(pack(u, a1, b1, la, jnp.zeros_like(la)), n_tgt), "tgt")
    tg = lax.all_gather(pack(v, a2, b2, lb, g), "src", axis=0)
    bs, bt = n_tgt, n_src
    rows, cols = bs * LANES, bt * LANES
    old = jnp.pad(old_moment, ((LATENT, LANES - LATENT - RANK),) * 2)

    lse, own, carried, xh, xl, rt, rc = call(
        functools.partial(old_kernel, n_tgt, bs),
        [
            ((n_tgt, bs, LANES), f32),
            ((bs, LANES), f32),
            ((rows, LANES), f32),
            ((FEAT, rows), bf16),
            ((FEAT, rows), bf16),
            ((DEPTH, cols), bf16),
            ((cols, DEPTH), bf16),
        ],
        [((rows, DEPTH), bf16), ((cols, LANES), bf16)],
        name="old_plan",
    )(sg, tg, old)
    f, moment = call(
        functools.partial(moment_kernel, n_tgt, bs),
        [((bs, LANES), f32), ((n_tgt, PACK - ROW_RIGHT, LANES), f32)],
        name="moment",
    )(swap(lse, "tgt"), own, carried, sg)
    (moment,) = call(
        functools.partial(sum_kernel, n_src),
        [((n_src, PACK - ROW_RIGHT, LANES), f32)],
        name="moment_sum",
    )(swap(moment, "tgt"))
    part, lc, lt = call(
        functools.partial(first_g_kernel, n_src, bs),
        [((n_src, bt, LANES), f32), ((rows, DEPTH), bf16), ((DEPTH, rows), bf16)],
        name="first_g",
    )(swap(moment, "src"), f, xh, xl, rc)
    half = lambda n, b, cells, name: call(
        functools.partial(half_kernel, n, b),
        [((n, b, LANES), f32), ((b, LANES), f32)],
        [((DEPTH, cells), bf16)],
        name=name,
    )
    part, _ = half(n_tgt, bt, cols, "first_f")(swap(part, "src"), tg, lc, rt)
    part, _ = half(n_src, bs, rows, "second_g")(swap(part, "tgt"), sg, rc, lt)
    part, g = half(n_tgt, bt, cols, "second_f")(swap(part, "src"), tg, lc, rt)
    (f,) = call(functools.partial(last_kernel, bs), [((bs, LANES), f32)], name="last_f")(swap(part, "tgt"), sg)
    return f.reshape(-1), g.reshape(-1)


def solution(mesh):
    return jax.shard_map(
        functools.partial(shards, mesh.shape["src"], mesh.shape["tgt"]),
        mesh=mesh,
        in_specs=(
            P(("src", "tgt"), None),
            P(("src", "tgt"), None),
            P(("src", "tgt"), None),
            P(("src", "tgt")),
            P("tgt", "src", None, None),
            P("tgt", "src", None, None),
            P("tgt", "src", None, None),
            P("tgt", "src", None),
            P("tgt", "src", None),
            P(),
        ),
        out_specs=(P("src"), P("tgt")),
        check_vma=False,
    )
```

time: 731 us -> 180 us (0.25)
  blocking collectives: 540 us -> 110 us
  other arithmetic: 64.9 us -> 0 us
  matrix products: 58.3 us -> 0 us
  Pallas kernels: 0 us -> 53.5 us
  waiting for transfers between devices: 51.6 us -> 0.01 us
  between operations: 14.4 us -> 0.73 us
  starting transfers between devices: 0.04 us -> 7.61 us
    psum x6 -> x0, blocking collectives: 210 us -> none  [the longest x3 115 us: row_lse(): total = lax.psum(jnp.sum(jnp.exp(scores - top[:, None]), axis=1), 'tgt')]
    pmax x5 -> x0, blocking collectives: 159 us -> none  [the longest x3 111 us: row_lse(): top = lax.pmax(jnp.max(scores, axis=1), 'tgt')]
    all_gather x9 -> x1, blocking collectives: 171 us -> 22.5 us  [shards(): tg = lax.all_gather(pack(v, a2, b2, lb, g), 'src', axis=0)]
    all_to_all x0 -> x7, blocking collectives: none -> 87.6 us  [swap(): return lax.all_to_all(x, axis, 0, 0)]
    dot_general x6 -> x0, matrix products: 58.3 us -> none  [the longest x2 37.6 us: build_cost(): lax.dot_general(left, right, (((1,), (1,)), ((), ())), precision=lax.Prec...]
    pallas_call x0 -> x8, Pallas kernels: none -> 53.5 us  [call(): pl.pallas_call(kernel, out_shape=[jax.ShapeDtypeStruct(s, d) for s, d in...]
    psum x1 -> x0, waiting for transfers between devices: 51.6 us -> none  [shards(): summed = lax.psum(carried, 'tgt')]
    reduce_sum x6 -> x0, other arithmetic: 41.8 us -> none  [the longest x3 25.8 us: row_lse(): total = lax.psum(jnp.sum(jnp.exp(scores - top[:, None]), axis=1), 'tgt')]
  transfers between devices with their start and end apart: 1 -> 1, of which waited for: 1 -> 0; matrix products, arithmetic and copies ran while one was open for 0% -> 0% of each run, Pallas kernels for 0% -> 0%
where the time goes in v1:
time: 180 us; the launch traced here: 177 us
  blocking collectives  110 us (61%)
  Pallas kernels  53.5 us (30%)
  starting transfers between devices  7.61 us (4%)
  local copies, waits for them, and re-layouts  5.28 us (3%)
    all_to_all x7, blocking collectives, swap(): return lax.all_to_all(x, axis, 0, 0)  87.6 us
    pallas_call x8, Pallas kernels, call(): pl.pallas_call(kernel, out_shape=[jax.ShapeDtypeStruct(s, d) for s, d in...  53.5 us
    all_gather x1, blocking collectives, shards(): tg = lax.all_gather(pack(v, a2, b2, lb, g), 'src', axis=0)  22.5 us
    all_to_all x1, starting transfers between devices, swap(): return lax.all_to_all(x, axis, 0, 0)  7.61 us
  transfers between devices with their start and end apart: 1, of which 0 were waited for; matrix products, arithmetic and copies ran while one was open for 0% of the time, Pallas kernels for 0%

profile of v1, /device:TPU:2, one launch (start us, length us, event | category | flops | bytes accessed | tf_op | source)
XLA Modules:
  0.0 177.2 jit_solution(9754527169624581389)
XLA Ops:
  0.7 0.7 copy-done.3
  1.3 2.1 %concatenate.6 = f32[112,128]{1,0:T(8,128)S(1)} concatenate(f32[32,128]{1,0:T(8,128)S(1)} %bitcast.25, f32[34,128]{1,0:T(8,128)} %bitcast.23, f32[1,128]{1,0:T(1,128)} %bitcast.28, f32[1,128]{1,0:T(1,128)S(1)} %broadcast_in_dim_broadcast_in_dim.3, f32[4,128]{1,0:T(4,128)S(1)} %broadcast.9, f32[34,128]{1,0:T(8,128)} %bitcast.24, f32[6,128]{1,0:T(8,128)S(1)} %broadcast.10), dimensions={0} | concatenate | bytes 114688 | tf_op jit(solution)/shard_map/concatenate | solution.py:241
  3.5 1.0 broadcast_in_dim.10
  4.5 7.6 %all-to-all-start = ((f32[16,112,128]{2,1,0:T(8,128)}), f32[16,112,128]{2,1,0:T(8,128)S(1)}, u32[]{:S(2)}, u32[]{:S(2)}) async-start(f32[16,112,128]{2,1,0:T(8,128)} %broadcast_in_dim.10), calls=%async_computation | async-start | bytes 1835008 | tf_op jit(solution)/shard_map/all_to_all | solution.py:249
  12.1 0.0 copy-start.1
  12.1 0.1 pad.4.moment
  12.2 0.6 copy-done.1
  12.8 0.0 copy-done.2
  12.9 0.7 copy-done.4
  13.6 22.5 %all-gather = f32[1792,128]{1,0:T(8,128)S(1)} all-gather(f32[112,128]{1,0:T(8,128)S(1)} %concatenate.7), channel_id=2, replica_groups=mesh['src'=16,'tgt'=16] {'src'}, dimensions={0}, use_global_device_ids=true | all-gather | bytes 974848 | tf_op jit(solution)/shard_map/all_gather | solution.py:257
  36.1 15.8 %old_plan.1 = (f32[16,16,128]{2,1,0:T(8,128)S(1)}, f32[16,128]{1,0:T(8,128)S(1)}, f32[2048,128]{1,0:T(8,128)S(1)}, bf16[80,2048]{1,0:T(8,128)(2,1)S(1)}, bf16[80...) custom-call(f32[16,112,128]{2,1,0:T(8,128)S(1)} %all-to-all-done.sg.gathered, ...), custom_call_target="tpu_custom_call" | custom-call | tf_op jit(solution)/shard_map/old_plan/pallas_call | solution.py:227
  51.9 13.6 %all_to_all.40.parts = f32[16,16,128]{2,1,0:T(8,128)S(1)} all-to-all(f32[16,16,128]{2,1,0:T(8,128)S(1)} %get-tuple-element.18), channel_id=1, replica_groups=mesh['src'=16,'tgt'=16] {'tgt'}, dimensions={0} | all-to-all | bytes 262144 | tf_op jit(solution)/shard_map/all_to_all | solution.py:249
  65.5 0.6 moment.1
  66.1 12.1 %all_to_all.41.parts = f32[16,40,128]{2,1,0:T(8,128)S(1)} all-to-all(f32[16,40,128]{2,1,0:T(8,128)S(1)} %get-tuple-element.21), channel_id=1, replica_groups=mesh['src'=16,'tgt'=16] {'tgt'}, dimensions={0} | all-to-all | bytes 655360 | tf_op jit(solution)/shard_map/all_to_all | solution.py:249
  78.3 15.9 %all_to_all.42.parts = f32[16,40,128]{2,1,0:T(8,128)S(1)} all-to-all(f32[16,40,128]{2,1,0:T(8,128)S(1)} %moment_sum.1), channel_id=1, replica_groups=mesh['src'=16,'tgt'=16] {'src'}, dimensions={0} | all-to-all | bytes 655360 | tf_op jit(solution)/shard_map/all_to_all | solution.py:249
  94.2 9.7 %first_g.1 = (f32[16,16,128]{2,1,0:T(8,128)S(1)}, bf16[2048,256]{1,0:T(8,128)(2,1)S(1)}, bf16[256,2048]{1,0:T(8,128)(2,1)S(1)}) custom-call(f32[16,40,128]{2,1,0:T(8,128)S(1)} %all_to_all.42.parts, f32[16,128]{1,0:T(8,128)S(1)} %get-tuple-element.22.f, bf16[80,2048]{1,0:T(8,128)(2,1)S(1)} %get-tuple-element.23.xh, ...), custom_call_target="tpu_custom_call" | custom-call | tf_op jit(solution)/shard_map/first_g/pallas_call | solution.py:227
  103.9 12.2 %all_to_all.43.parts = f32[16,16,128]{2,1,0:T(8,128)S(1)} all-to-all(f32[16,16,128]{2,1,0:T(8,128)S(1)} %get-tuple-element.26), channel_id=1, replica_groups=mesh['src'=16,'tgt'=16] {'src'}, dimensions={0} | all-to-all | bytes 262144 | tf_op jit(solution)/shard_map/all_to_all | solution.py:249
  116.1 8.9 %first_f.1 = (f32[16,16,128]{2,1,0:T(8,128)S(1)}, f32[16,128]{1,0:T(8,128)}) custom-call(f32[16,16,128]{2,1,0:T(8,128)S(1)} %all_to_all.43.parts, f32[16,112,128]{2,1,0:T(8,128)S(1)} %bitcast.21, bf16[2048,256]{1,0:T(8,128)(2,1)S(1)} %get-tuple-element.27.stream, bf16[256,2048]{1,0:T(8,128)(2,1)S(1)} %get-tuple-element.28.fixed), custom_call_target="tpu_custom_call" | custom-call | tf_op jit(solution)/shard_map/first_f/pallas_call | solution.py:227
  125.0 11.1 %all_to_all.44.parts = f32[16,16,128]{2,1,0:T(8,128)S(1)} all-to-all(f32[16,16,128]{2,1,0:T(8,128)S(1)} %get-tuple-element.29), channel_id=1, replica_groups=mesh['src'=16,'tgt'=16] {'tgt'}, dimensions={0} | all-to-all | bytes 262144 | tf_op jit(solution)/shard_map/all_to_all | solution.py:249
  136.1 8.9 %second_g.1 = (f32[16,16,128]{2,1,0:T(8,128)S(1)}, f32[16,128]{1,0:T(8,128)}) custom-call(f32[16,16,128]{2,1,0:T(8,128)S(1)} %all_to_all.44.parts, f32[16,112,128]{2,1,0:T(8,128)S(1)} %all-to-all-done.sg.gathered, bf16[2048,256]{1,0:T(8,128)(2,1)S(1)} %get-tuple-element.25.rc.stream, bf16[256,2048]{1,0:T(8,128)(2,1)S(1)} %get-tuple-element.30.fixed), custom_call_target="tpu_custom_call" | custom-call | tf_op jit(solution)/shard_map/second_g/pallas_call | solution.py:227
  145.1 11.3 %all_to_all.45.parts = f32[16,16,128]{2,1,0:T(8,128)S(1)} all-to-all(f32[16,16,128]{2,1,0:T(8,128)S(1)} %get-tuple-element.31), channel_id=1, replica_groups=mesh['src'=16,'tgt'=16] {'src'}, dimensions={0} | all-to-all | bytes 262144 | tf_op jit(solution)/shard_map/all_to_all | solution.py:249
  156.3 8.9 %second_f.1 = (f32[16,16,128]{2,1,0:T(8,128)S(1)}, f32[16,128]{1,0:T(8,128)}) custom-call(f32[16,16,128]{2,1,0:T(8,128)S(1)} %all_to_all.45.parts, f32[16,112,128]{2,1,0:T(8,128)S(1)} %bitcast.22, bf16[2048,256]{1,0:T(8,128)(2,1)S(1)} %get-tuple-element.27.stream, bf16[256,2048]{1,0:T(8,128)(2,1)S(1)} %get-tuple-element.28.fixed), custom_call_target="tpu_custom_call" | custom-call | tf_op jit(solution)/shard_map/second_f/pallas_call | solution.py:227
  165.3 11.3 %all_to_all.46.parts = f32[16,16,128]{2,1,0:T(8,128)S(1)} all-to-all(f32[16,16,128]{2,1,0:T(8,128)S(1)} %get-tuple-element.32), channel_id=1, replica_groups=mesh['src'=16,'tgt'=16] {'tgt'}, dimensions={0} | all-to-all | bytes 262144 | tf_op jit(solution)/shard_map/all_to_all | solution.py:249
  176.6 0.7 last_f.1
  (16 shorter events, 0.1 us)
Async XLA Ops:
  0.6 0.7 copy-start.3
  4.5 7.6 %copy-start = (f32[34,34]{1,0:T(8,128)S(1)}, f32[34,34]{1,0:T(8,128)}, u32[]{:S(2)}) copy-start(f32[34,34]{1,0:T(8,128)} %param.19) | copy-start | bytes 13876
  4.5 31.6 %all-to-all-start = ((f32[16,112,128]{2,1,0:T(8,128)}), f32[16,112,128]{2,1,0:T(8,128)S(1)}, u32[]{:S(2)}, u32[]{:S(2)}) async-start(f32[16,112,128]{2,1,0:T(8,128)} %broadcast_in_dim.10), calls=%async_computation | async-start | bytes 1835008 | tf_op jit(solution)/shard_map/all_to_all | solution.py:249
  12.1 0.7 copy-start.1
  12.1 0.7 copy-start.2
  12.8 0.7 copy-start.4
  12.8 0.7 copy-start.5
  12.8 0.7 copy-start.6

commit v2 on v1

v2 whole, which is shorter than its diff:
```python
import functools

import jax
import jax.numpy as jnp
from jax import lax
from jax.experimental import pallas as pl
from jax.experimental.pallas import tpu as pltpu
from jax.sharding import PartitionSpec as P

LATENT = 32
RANK = 34
FEAT = 80
BIAS = 3 * FEAT
DEPTH = 256
LANES = 128
ENTROPY = 0.1
LOG2E = 1.4426950408889634
SCALE = LOG2E / ENTROPY

ROW_LOGW = LATENT + RANK
ROW_POT = ROW_LOGW + 1
ROW_RIGHT = 72
PACK = 112
RIGHT = 48
MOMENT = 40
CHUNK = 256

f32 = jnp.float32
bf16 = jnp.bfloat16


def dot(a, b):
    return jnp.dot(a, b, preferred_element_type=f32)


def dot_nt(a, b):
    return lax.dot_general(a, b, (((1,), (1,)), ((), ())), preferred_element_type=f32)


def split(x):
    hi = x.astype(bf16)
    return hi, (x - hi.astype(f32)).astype(bf16)


def iota(shape, axis):
    return lax.broadcasted_iota(jnp.int32, shape, axis)


def eye():
    shape = (LANES, LANES)
    return iota(shape, 0) == iota(shape, 1)


def to_lanes(column, mask):
    return jnp.sum(jnp.where(mask, column, 0.0), axis=0, keepdims=True)


def tile(t):
    return slice(t * LANES, (t + 1) * LANES)


def features(block):
    x = block[0:FEAT]
    return jnp.where(iota(x.shape, 0) < LATENT + RANK, x, 0.0)


def pick(x, row, n):
    return jnp.concatenate([x[t, row : row + 1, :] for t in range(n)], axis=0)


def half_square(block):
    x = block[0:LATENT]
    return 0.5 * jnp.sum(x * x, axis=0, keepdims=True)


def three(x):
    hi = x.astype(bf16).astype(f32)
    rest = x - hi
    mid = rest.astype(bf16).astype(f32)
    return hi, mid, rest - mid


def extra(terms):
    rows = iota((DEPTH - BIAS, LANES), 0)
    out = jnp.zeros(rows.shape, f32)
    for k, x in terms.items():
        out = jnp.where(rows == k, x, out)
    return out.astype(bf16)


ONES = {0: 1.0, 1: 1.0, 2: 1.0}


def put_bias(ref, potential):
    for t in range(potential.shape[0]):
        ref[BIAS:DEPTH, tile(t)] = extra(dict(enumerate(three(potential[t : t + 1]))))


def left_operand(xh, xl, moment):
    shape = (LANES, LANES)
    row, column = iota(shape, 0), iota(shape, 1)
    mixed = moment.T + jnp.where((row == column) & (row < LATENT), 1.0, 0.0)
    qh, ql = split((SCALE * mixed)[0:FEAT, 0:FEAT])
    both = dot(jnp.concatenate([qh, ql], axis=0), xh)
    return split(both[0:FEAT] + both[FEAT:] + dot(qh, xl))


def transpose_into(ref, t, block):
    unit = jnp.where(eye(), 1.0, 0.0).astype(bf16)
    ref[tile(t), :] = dot_nt(unit, block).astype(bf16)


def reduce_rows(s, row, mask):
    tops, totals = [], []
    for k in range(0, LANES, 8):
        x = [s[row + k : row + k + 8, tile(t)] for t in range(s.shape[1] // LANES)]
        top = functools.reduce(jnp.maximum, x)
        tops.append(top)
        totals.append(functools.reduce(jnp.add, [jnp.exp2(y - top) for y in x]))
    top, total = jnp.concatenate(tops, axis=0), jnp.concatenate(totals, axis=0)
    whole = jnp.max(top, axis=1, keepdims=True)
    total = jnp.sum(total * jnp.exp2(top - whole), axis=1, keepdims=True)
    return to_lanes(whole + jnp.log2(total), mask)


def lse_rows(stream, fixed, out_ref, n, s0, s1, held):
    mask = eye()
    s = (s0, s1)
    steps = stream.shape[0] // CHUNK
    s0[...] = dot(stream[0:CHUNK, :], fixed[...])
    for b in range(steps):
        if b + 1 < steps:
            s[(b + 1) % 2][...] = dot(stream[(b + 1) * CHUNK : (b + 2) * CHUNK, :], fixed[...])
        for k in range(CHUNK // LANES):
            t = b * (CHUNK // LANES) + k
            held[t : t + 1, :] = reduce_rows(s[b % 2], k * LANES, mask)
    for k in range(n):
        out_ref[k] = held[...]


def combine(parts):
    top = jnp.max(parts, axis=0)
    return top + jnp.log2(jnp.sum(jnp.exp2(parts - top[None]), axis=0))


def pack_kernel(n, u, a1, b1, la, v, a2, b2, lb, g, source, target):
    def rows(latent, left, right, logw, pot):
        return [
            (0, latent[...]),
            (LATENT, left[...]),
            (ROW_LOGW, logw[...]),
            (ROW_POT, pot),
            (ROW_POT + 1, jnp.zeros((ROW_RIGHT - ROW_POT - 1, LANES), f32)),
            (ROW_RIGHT, right[...]),
            (ROW_RIGHT + RANK, jnp.zeros((PACK - ROW_RIGHT - RANK, LANES), f32)),
        ]

    for at, x in rows(v, a2, b2, lb, g[...]):
        target[at : at + x.shape[0], :] = x
    for at, x in rows(u, a1, b1, la, jnp.zeros((1, LANES), f32)):
        for k in range(n):
            source[k, at : at + x.shape[0], :] = x


def old_kernel(n, blocks, sg, tg, moment, lse_out, lse_own, carried, xh, xl, rt, rc, lt, b2, s0, s1, ph, pl_, held):
    for t in range(blocks):
        hi, low = split(features(tg[t]))
        rt[0:FEAT, tile(t)] = hi
        rt[FEAT : 2 * FEAT, tile(t)] = low
        rt[2 * FEAT : BIAS, tile(t)] = hi
        pot = SCALE * (tg[t, ROW_POT : ROW_POT + 1, :] - half_square(tg[t]))
        more = extra(ONES | {3 + k: x for k, x in enumerate(three(pot))})
        transpose_into(rc, t, jnp.concatenate([hi, low, hi, more], axis=0))
        right = jnp.concatenate([tg[t, ROW_RIGHT:PACK, :], jnp.zeros((RIGHT + ROW_RIGHT - PACK, LANES), f32)], axis=0)
        hi, low = split(right)
        b2[0:RIGHT, tile(t)] = hi
        b2[RIGHT:, tile(t)] = low
        hi, low = split(features(sg[t]))
        xh[:, tile(t)] = hi
        xl[:, tile(t)] = low
        lt[BIAS:DEPTH, tile(t)] = extra({3: 1.0, 4: 1.0, 5: 1.0})
    lh, ll = left_operand(xh[...], xl[...], moment[...])
    lt[0:FEAT, :] = lh
    lt[FEAT : 2 * FEAT, :] = lh
    lt[2 * FEAT : BIAS, :] = ll
    cells, piece = rc.shape[0], 64
    steps = lt.shape[1] // CHUNK

    def columns(b):
        return pl.ds(pl.multiple_of(b * CHUNK, CHUNK), CHUNK)

    def scores(b, s):
        s[...] = dot(rc[...], lt[:, columns(b)])

    def plan(b, s):
        top = s[0:piece, :]
        for k in range(piece, cells, piece):
            top = jnp.maximum(top, s[k : k + piece, :])
        top = jnp.max(top, axis=0, keepdims=True)
        total = jnp.zeros((piece, CHUNK), f32)
        for k in range(0, cells, piece):
            p = jnp.exp2(s[k : k + piece, :] - top)
            total = total + p
            hi, low = split(p)
            ph[k : k + piece, :] = hi
            pl_[k : k + piece, :] = low
        total = jnp.sum(total, axis=0, keepdims=True)
        c = dot(b2[...], ph[...])
        c = c[0:RIGHT] + c[RIGHT:] + dot(b2[0:RIGHT, :], pl_[...])
        carried[:, columns(b)] = c / total
        held[:, columns(b)] = top + jnp.log2(total)

    scores(0, s0)

    def step(i, carry):
        scores(2 * i + 1, s1)
        plan(2 * i, s0)
        scores(lax.rem(2 * i + 2, steps), s0)
        plan(2 * i + 1, s1)
        return carry

    lax.fori_loop(0, steps // 2, step, 0)
    lse = jnp.concatenate([held[:, tile(t)] for t in range(cells // LANES)], axis=0)
    lse_own[...] = lse
    for k in range(n):
        lse_out[k] = lse


def moment_kernel(n, blocks, parts, lse_own, carried, sg, f_out, moment_out):
    f = LOG2E * pick(sg, ROW_LOGW, blocks) - combine(parts[...])
    f_out[...] = f
    weight = jnp.exp2(f + lse_own[...])
    left = [sg[t, ROW_RIGHT:PACK, :] * weight[t : t + 1] for t in range(blocks)]
    hi, low = split(jnp.concatenate(left, axis=1))
    ch, cl = split(carried[...])
    fill = jnp.zeros((LANES - RIGHT, ch.shape[1]), bf16)
    ch, cl = jnp.concatenate([ch, fill], axis=0), jnp.concatenate([cl, fill], axis=0)
    x = dot_nt(hi, ch) + dot_nt(low, ch) + dot_nt(hi, cl)
    second, third = pltpu.roll(x[16:32], MOMENT, 1), pltpu.roll(x[32:40], 2 * MOMENT, 1)
    packed = x[0:16] + second + jnp.concatenate([third, jnp.zeros_like(third)], axis=0)
    for k in range(n):
        moment_out[k] = packed


def sum_kernel(n, parts, out):
    total = jnp.sum(parts[...], axis=0)
    for k in range(n):
        out[k] = total


def unpack_moment(packed):
    first = pltpu.roll(packed, LATENT, 1)
    second = pltpu.roll(packed, LANES + LATENT - MOMENT, 1)
    third = pltpu.roll(packed[0:8], LANES + LATENT - 2 * MOMENT, 1)
    x = jnp.concatenate([first, second, third], axis=0)
    rows, lanes = iota(x.shape, 0), iota(x.shape, 1)
    x = jnp.where((rows < RANK) & (lanes >= LATENT) & (lanes < LATENT + RANK), x, 0.0)
    return jnp.concatenate([jnp.zeros((LATENT, LANES), f32), x, jnp.zeros((LANES - LATENT - MOMENT, LANES), f32)], axis=0)


def first_g_kernel(n, blocks, parts, f, xh, xl, rc, out, lc, lt, s0, s1, held):
    moment = unpack_moment(jnp.sum(parts[...], axis=0))
    lh, ll = left_operand(xh[...], xl[...], moment)
    lt[0:FEAT, :] = lh
    lt[FEAT : 2 * FEAT, :] = lh
    lt[2 * FEAT : BIAS, :] = ll
    put_bias(lt, f[...])
    for t in range(blocks):
        transpose_into(lc, t, jnp.concatenate([lt[0:BIAS, tile(t)], extra(ONES)], axis=0))
    lse_rows(rc, lt, out, n, s0, s1, held)


def potential(blocks, parts, gathered):
    x = LOG2E * pick(gathered, ROW_LOGW, blocks) - combine(parts[...])
    square = jnp.concatenate([half_square(gathered[t]) for t in range(blocks)], axis=0)
    return x, x * (1.0 / SCALE) + square


def half_kernel(n, blocks, parts, gathered, stream, fixed_in, out, pot_out, fixed, s0, s1, held):
    x, pot_out[...] = potential(blocks, parts, gathered)
    put_bias(fixed, x)
    lse_rows(stream, fixed, out, n, s0, s1, held)


def last_kernel(blocks, parts, gathered, pot_out):
    _, pot_out[...] = potential(blocks, parts, gathered)


def call(kernel, out, scratch=(), name=None, aliases={}):
    spec = pl.BlockSpec(memory_space=pltpu.VMEM)
    return lambda *args: pl.pallas_call(
        kernel,
        out_shape=[jax.ShapeDtypeStruct(s, d) for s, d in out],
        in_specs=[spec] * len(args),
        out_specs=[spec] * len(out),
        scratch_shapes=[pltpu.VMEM(s, d) for s, d in scratch],
        input_output_aliases=aliases,
        compiler_params=pltpu.CompilerParams(vmem_limit_bytes=32 * 1024 * 1024),
        name=name,
    )(*args)


def swap(x, axis):
    return lax.all_to_all(x, axis, 0, 0)


def shards(n_src, n_tgt, *args):
    (u, a1, b1, la, v, a2, b2, lb, g, old_moment) = args
    v, a2, b2 = (x.reshape(-1, x.shape[-1]) for x in (v, a2, b2))
    flat = lambda x: x.reshape(1, -1)
    source, target = call(
        functools.partial(pack_kernel, n_tgt),
        [((n_tgt, PACK, LANES), f32), ((PACK, LANES), f32)],
        name="pack",
    )(u.T, a1.T, b1.T, flat(la), v.T, a2.T, b2.T, flat(lb), flat(g))
    sg = swap(source, "tgt")
    tg = lax.all_gather(target, "src", axis=0)
    bs, bt = n_tgt, n_src
    rows, cols = bs * LANES, bt * LANES
    old = jnp.pad(old_moment, ((LATENT, LANES - LATENT - RANK),) * 2)

    lse, own, carried, xh, xl, rt, rc = call(
        functools.partial(old_kernel, n_tgt, bs),
        [
            ((n_tgt, bs, LANES), f32),
            ((bs, LANES), f32),
            ((RIGHT, rows), f32),
            ((FEAT, rows), bf16),
            ((FEAT, rows), bf16),
            ((DEPTH, cols), bf16),
            ((cols, DEPTH), bf16),
        ],
        [
            ((DEPTH, rows), bf16),
            ((2 * RIGHT, cols), bf16),
            ((cols, CHUNK), f32),
            ((cols, CHUNK), f32),
            ((cols, CHUNK), bf16),
            ((cols, CHUNK), bf16),
            ((1, rows), f32),
        ],
        name="old_plan",
    )(sg, tg, old)
    f, moment = call(
        functools.partial(moment_kernel, n_tgt, bs),
        [((bs, LANES), f32), ((n_tgt, 16, LANES), f32)],
        name="moment",
    )(swap(lse, "tgt"), own, carried, sg)
    (moment,) = call(functools.partial(sum_kernel, n_src), [((n_src, 16, LANES), f32)], name="moment_sum")(
        swap(moment, "tgt")
    )
    pipe = lambda cells, b: [((CHUNK, cells), f32), ((CHUNK, cells), f32), ((b, LANES), f32)]
    part, lc, lt = call(
        functools.partial(first_g_kernel, n_src, bs),
        [((n_src, bt, LANES), f32), ((rows, DEPTH), bf16), ((DEPTH, rows), bf16)],
        pipe(rows, bt),
        name="first_g",
    )(swap(moment, "src"), f, xh, xl, rc)
    half = lambda n, fixed, streamed, name: call(
        functools.partial(half_kernel, n, fixed),
        [((n, streamed, LANES), f32), ((fixed, LANES), f32), ((DEPTH, fixed * LANES), bf16)],
        pipe(fixed * LANES, streamed),
        name=name,
        aliases={3: 2},
    )
    part, _, rt = half(n_tgt, bt, bs, "first_f")(swap(part, "src"), tg, lc, rt)
    part, _, lt = half(n_src, bs, bt, "second_g")(swap(part, "tgt"), sg, rc, lt)
    part, g, rt = half(n_tgt, bt, bs, "second_f")(swap(part, "src"), tg, lc, rt)
    (f,) = call(functools.partial(last_kernel, bs), [((bs, LANES), f32)], name="last_f")(swap(part, "tgt"), sg)
    return f.reshape(-1), g.reshape(-1)


def solution(mesh):
    return jax.shard_map(
        functools.partial(shards, mesh.shape["src"], mesh.shape["tgt"]),
        mesh=mesh,
        in_specs=(
            P(("src", "tgt"), None),
            P(("src", "tgt"), None),
            P(("src", "tgt"), None),
            P(("src", "tgt")),
            P("tgt", "src", None, None),
            P("tgt", "src", None, None),
            P("tgt", "src", None, None),
            P("tgt", "src", None),
            P("tgt", "src", None),
            P(),
        ),
        out_specs=(P("src"), P("tgt")),
        check_vma=False,
    )
```

time: 180 us -> 147 us (0.82)
  Pallas kernels: 53.5 us -> 30.1 us
  blocking collectives: 110 us -> 105 us
  local copies, waits for them, and re-layouts: 5.28 us -> 1.53 us
    pallas_call x8 -> x9, Pallas kernels: 53.5 us -> 30.1 us  [call(): pl.pallas_call(kernel, out_shape=[jax.ShapeDtypeStruct(s, d) for s, d in...]
    all_to_all x7, blocking collectives: 87.6 us -> 82.6 us  [swap(): return lax.all_to_all(x, axis, 0, 0)]
    concatenate x2 -> x0, local copies, waits for them, and re-layouts: 2.17 us -> none  [pack(): jnp.concatenate(rows + [right.T, jnp.zeros((PACK - ROW_RIGHT - RANK, cell...]
where the time goes in v2:
time: 147 us; the launch traced here: 145 us
  blocking collectives  105 us (71%)
  Pallas kernels  30.1 us (20%)
  starting transfers between devices  7.61 us (5%)
  local copies, waits for them, and re-layouts  1.53 us (1%)
    all_to_all x7, blocking collectives, swap(): return lax.all_to_all(x, axis, 0, 0)  82.6 us
    pallas_call x9, Pallas kernels, call(): pl.pallas_call(kernel, out_shape=[jax.ShapeDtypeStruct(s, d) for s, d in...  30.1 us
    all_gather x1, blocking collectives, shards(): tg = lax.all_gather(target, 'src', axis=0)  22.5 us
    all_to_all x1, starting transfers between devices, swap(): return lax.all_to_all(x, axis, 0, 0)  7.61 us
  transfers between devices with their start and end apart: 1, of which 0 were waited for; matrix products, arithmetic and copies ran while one was open for 0% of the time, Pallas kernels for 0%

profile of v2, /device:TPU:2, one launch (start us, length us, event | category | flops | bytes accessed | tf_op | source)
XLA Modules:
  0.0 145.1 jit_solution(14033868157092976898)
XLA Ops:
  0.6 0.0 copy-start
  0.6 0.0 copy-start.1
  0.7 0.0 copy-start.3
  0.7 0.8 copy_bitcast_fusion
  1.5 0.7 copy-done.2
  2.2 1.0 pack.1
  3.2 7.6 %all-to-all-start = ((f32[16,112,128]{2,1,0:T(8,128)}), f32[16,112,128]{2,1,0:T(8,128)S(1)}, u32[]{:S(2)}, u32[]{:S(2)}) async-start(f32[16,112,128]{2,1,0:T(8,128)} %get-tuple-element.21), calls=%async_computation | async-start | bytes 1835008 | tf_op jit(solution)/shard_map/all_to_all | solution.py:304
  10.8 0.1 pad.4.moment
  10.9 22.5 %all-gather = f32[1792,128]{1,0:T(8,128)S(1)} all-gather(f32[112,128]{1,0:T(8,128)S(1)} %get-tuple-element.22), channel_id=2, replica_groups=mesh['src'=16,'tgt'=16] {'src'}, dimensions={0}, use_global_device_ids=true | all-gather | bytes 974848 | tf_op jit(solution)/shard_map/all_gather | solution.py:317
  33.3 0.0 all-to-all-done.sg.gathered
  33.3 8.8 %old_plan.1 = (f32[16,16,128]{2,1,0:T(8,128)S(1)}, f32[16,128]{1,0:T(8,128)S(1)}, f32[48,2048]{1,0:T(8,128)S(1)}, bf16[80,2048]{1,0:T(8,128)(2,1)S(1)}, bf16[80,...) custom-call(f32[16,112,128]{2,1,0:T(8,128)S(1)} %all-to-all-done.sg.gathered, ...), custom_call_target="tpu_custom_call" | custom-call | tf_op jit(solution)/shard_map/old_plan/pallas_call | solution.py:291
  42.1 13.6 %all_to_all.40.parts = f32[16,16,128]{2,1,0:T(8,128)S(1)} all-to-all(f32[16,16,128]{2,1,0:T(8,128)S(1)} %get-tuple-element.23), channel_id=1, replica_groups=mesh['src'=16,'tgt'=16] {'tgt'}, dimensions={0} | all-to-all | bytes 262144 | tf_op jit(solution)/shard_map/all_to_all | solution.py:304
  55.7 0.4 moment.1
  56.2 11.1 %all_to_all.41.parts = f32[16,16,128]{2,1,0:T(8,128)S(1)} all-to-all(f32[16,16,128]{2,1,0:T(8,128)S(1)} %get-tuple-element.26), channel_id=1, replica_groups=mesh['src'=16,'tgt'=16] {'tgt'}, dimensions={0} | all-to-all | bytes 262144 | tf_op jit(solution)/shard_map/all_to_all | solution.py:304
  67.3 12.3 %all_to_all.42.parts = f32[16,16,128]{2,1,0:T(8,128)S(1)} all-to-all(f32[16,16,128]{2,1,0:T(8,128)S(1)} %moment_sum.1), channel_id=1, replica_groups=mesh['src'=16,'tgt'=16] {'src'}, dimensions={0} | all-to-all | bytes 262144 | tf_op jit(solution)/shard_map/all_to_all | solution.py:304
  79.5 4.9 %first_g.1 = (f32[16,16,128]{2,1,0:T(8,128)S(1)}, bf16[2048,256]{1,0:T(8,128)(2,1)S(1)}, bf16[256,2048]{1,0:T(8,128)(2,1)S(1)}) custom-call(f32[16,16,128]{2,1,0:T(8,128)S(1)} %all_to_all.42.parts, f32[16,128]{1,0:T(8,128)S(1)} %get-tuple-element.27.f, bf16[80,2048]{1,0:T(8,128)(2,1)S(1)} %get-tuple-element.28.xh, ...), custom_call_target="tpu_custom_call" | custom-call | tf_op jit(solution)/shard_map/first_g/pallas_call | solution.py:291
  84.4 11.7 %all_to_all.43.parts = f32[16,16,128]{2,1,0:T(8,128)S(1)} all-to-all(f32[16,16,128]{2,1,0:T(8,128)S(1)} %get-tuple-element.31), channel_id=1, replica_groups=mesh['src'=16,'tgt'=16] {'src'}, dimensions={0} | all-to-all | bytes 262144 | tf_op jit(solution)/shard_map/all_to_all | solution.py:304
  96.1 4.8 %first_f.1 = (f32[16,16,128]{2,1,0:T(8,128)S(1)}, f32[16,128]{1,0:T(8,128)}, bf16[256,2048]{1,0:T(8,128)(2,1)S(1)}) custom-call(f32[16,16,128]{2,1,0:T(8,128)S(1)} %all_to_all.43.parts, f32[16,112,128]{2,1,0:T(8,128)S(1)} %bitcast.21, bf16[2048,256]{1,0:T(8,128)(2,1)S(1)} %get-tuple-element.32.stream, ...), custom_call_target="tpu_custom_call", output_to_operand_aliasing={{2}: (3, {})} | custom-call | tf_op jit(solution)/shard_map/first_f/pallas_call | solution.py:291
  100.9 11.1 %all_to_all.44.parts = f32[16,16,128]{2,1,0:T(8,128)S(1)} all-to-all(f32[16,16,128]{2,1,0:T(8,128)S(1)} %get-tuple-element.34), channel_id=1, replica_groups=mesh['src'=16,'tgt'=16] {'tgt'}, dimensions={0} | all-to-all | bytes 262144 | tf_op jit(solution)/shard_map/all_to_all | solution.py:304
  112.0 4.7 %second_g.1 = (f32[16,16,128]{2,1,0:T(8,128)S(1)}, f32[16,128]{1,0:T(8,128)}, bf16[256,2048]{1,0:T(8,128)(2,1)S(1)}) custom-call(f32[16,16,128]{2,1,0:T(8,128)S(1)} %all_to_all.44.parts, f32[16,112,128]{2,1,0:T(8,128)S(1)} %all-to-all-done.sg.gathered, bf16[2048,256]{1,0:T(8,128)(2,1)S(1)} %get-tuple-element.30.rc.stream, ...), custom_call_target="tpu_custom_call", output_to_operand_aliasing={{2}: (3, {})} | custom-call | tf_op jit(solution)/shard_map/second_g/pallas_call | solution.py:291
  116.7 11.5 %all_to_all.45.parts = f32[16,16,128]{2,1,0:T(8,128)S(1)} all-to-all(f32[16,16,128]{2,1,0:T(8,128)S(1)} %get-tuple-element.36), channel_id=1, replica_groups=mesh['src'=16,'tgt'=16] {'src'}, dimensions={0} | all-to-all | bytes 262144 | tf_op jit(solution)/shard_map/all_to_all | solution.py:304
  128.2 4.8 %second_f.1 = (f32[16,16,128]{2,1,0:T(8,128)S(1)}, f32[16,128]{1,0:T(8,128)}, bf16[256,2048]{1,0:T(8,128)(2,1)S(1)}) custom-call(f32[16,16,128]{2,1,0:T(8,128)S(1)} %all_to_all.45.parts, f32[16,112,128]{2,1,0:T(8,128)S(1)} %bitcast.22, bf16[2048,256]{1,0:T(8,128)(2,1)S(1)} %get-tuple-element.32.stream, ...), custom_call_target="tpu_custom_call", output_to_operand_aliasing={{2}: (3, {})} | custom-call | tf_op jit(solution)/shard_map/second_f/pallas_call | solution.py:291
  133.1 11.3 %all_to_all.46.parts = f32[16,16,128]{2,1,0:T(8,128)S(1)} all-to-all(f32[16,16,128]{2,1,0:T(8,128)S(1)} %get-tuple-element.38), channel_id=1, replica_groups=mesh['src'=16,'tgt'=16] {'tgt'}, dimensions={0} | all-to-all | bytes 262144 | tf_op jit(solution)/shard_map/all_to_all | solution.py:304
  144.4 0.7 last_f.1
  (13 shorter events, 0.0 us)
Async XLA Ops:
  0.6 0.8 copy-start
  0.6 0.8 copy-start.1
  0.7 0.8 copy-start.3
  0.7 0.8 copy-start.6
  1.4 0.7 copy-start.2
  1.4 0.7 copy-start.4
  1.4 0.7 copy-start.5
  3.2 7.6 %copy-start.7 = (f32[34,34]{1,0:T(8,128)S(1)}, f32[34,34]{1,0:T(8,128)}, u32[]{:S(2)}) copy-start(f32[34,34]{1,0:T(8,128)} %param.19) | copy-start | bytes 13876
  3.2 30.2 %all-to-all-start = ((f32[16,112,128]{2,1,0:T(8,128)}), f32[16,112,128]{2,1,0:T(8,128)S(1)}, u32[]{:S(2)}, u32[]{:S(2)}) async-start(f32[16,112,128]{2,1,0:T(8,128)} %get-tuple-element.21), calls=%async_computation | async-start | bytes 1835008 | tf_op jit(solution)/shard_map/all_to_all | solution.py:304

commit v3 on v2

--- a/solution.py
+++ b/solution.py
@@ -24,6 +24,9 @@
 RIGHT = 48
 MOMENT = 40
 CHUNK = 256
+HEADROOM = 100.0
+SMALLEST = 2.0**-99
+LARGEST = 2.0**126
 
 f32 = jnp.float32
 bf16 = jnp.bfloat16
@@ -91,9 +94,13 @@
 ONES = {0: 1.0, 1: 1.0, 2: 1.0}
 
 
-def put_bias(ref, potential):
+def put_bias(ref, potential, more={}):
     for t in range(potential.shape[0]):
-        ref[BIAS:DEPTH, tile(t)] = extra(dict(enumerate(three(potential[t : t + 1]))))
+        ref[BIAS:DEPTH, tile(t)] = extra(dict(enumerate(three(potential[t : t + 1]))) | more)
+
+
+def shifted(shift):
+    return extra(ONES | {3 + k: x for k, x in enumerate(three(shift))})
 
 
 def left_operand(xh, xl, moment):
@@ -108,6 +115,12 @@
 def transpose_into(ref, t, block):
     unit = jnp.where(eye(), 1.0, 0.0).astype(bf16)
     ref[tile(t), :] = dot_nt(unit, block).astype(bf16)
+
+
+def restream(ref, t, fixed, shift):
+    unit = jnp.where(eye(), 1.0, 0.0).astype(bf16)
+    block = jnp.concatenate([fixed[LANES:BIAS, tile(t)], shifted(shift)], axis=0)
+    ref[tile(t), LANES:DEPTH] = dot_nt(unit, block).astype(bf16)
 
 
 def reduce_rows(s, row, mask):
@@ -120,11 +133,18 @@
     top, total = jnp.concatenate(tops, axis=0), jnp.concatenate(totals, axis=0)
     whole = jnp.max(top, axis=1, keepdims=True)
     total = jnp.sum(total * jnp.exp2(top - whole), axis=1, keepdims=True)
-    return to_lanes(whole + jnp.log2(total), mask)
-
-
-def lse_rows(stream, fixed, out_ref, n, s0, s1, held):
-    mask = eye()
+    return to_lanes(whole, mask), to_lanes(total, mask)
+
+
+def add_rows(s, row, mask):
+    totals = []
+    for k in range(0, LANES, 8):
+        x = [jnp.exp2(s[row + k : row + k + 8, tile(t)]) for t in range(s.shape[1] // LANES)]
+        totals.append(functools.reduce(jnp.add, x))
+    return to_lanes(jnp.sum(jnp.concatenate(totals, axis=0), axis=1, keepdims=True), mask)
+
+
+def pipeline(stream, fixed, s0, s1, reduce):
     s = (s0, s1)
     steps = stream.shape[0] // CHUNK
     s0[...] = dot(stream[0:CHUNK, :], fixed[...])
@@ -132,10 +152,45 @@
         if b + 1 < steps:
             s[(b + 1) % 2][...] = dot(stream[(b + 1) * CHUNK : (b + 2) * CHUNK, :], fixed[...])
         for k in range(CHUNK // LANES):
-            t = b * (CHUNK // LANES) + k
-            held[t : t + 1, :] = reduce_rows(s[b % 2], k * LANES, mask)
-    for k in range(n):
-        out_ref[k] = held[...]
+            reduce(b * (CHUNK // LANES) + k, s[b % 2], k * LANES)
+
+
+def lse_rows(stream, fixed, out_ref, n, s0, s1, tops, totals):
+    mask = eye()
+
+    def reduce(t, s, row):
+        tops[t : t + 1, :], totals[t : t + 1, :] = reduce_rows(s, row, mask)
+
+    pipeline(stream, fixed, s0, s1, reduce)
+    lse = tops[...] + jnp.log2(totals[...])
+    for k in range(n):
+        out_ref[k] = lse
+
+
+def shifted_lse_rows(stream, fixed, shift, out_ref, n, s0, s1, tops, totals):
+    mask = eye()
+
+    def reduce(t, s, row):
+        totals[t : t + 1, :] = add_rows(s, row, mask)
+
+    pipeline(stream, fixed, s0, s1, reduce)
+    total = totals[...]
+    tops[...] = jnp.log2(total)
+    good = jnp.all((total >= SMALLEST) & (total <= LARGEST))
+
+    @pl.when(jnp.logical_not(good))
+    def _():
+        def step(t, carry):
+            s0[0:LANES, :] = dot(stream[pl.ds(pl.multiple_of(t * LANES, LANES), LANES), :], fixed[...])
+            top, total = reduce_rows(s0, 0, mask)
+            tops[pl.ds(t, 1), :] = top + jnp.log2(total)
+            return carry
+
+        lax.fori_loop(0, stream.shape[0] // LANES, step, 0)
+
+    lse = tops[...] - shift
+    for k in range(n):
+        out_ref[k] = lse
 
 
 def combine(parts):
@@ -145,21 +200,14 @@
 
 def pack_kernel(n, u, a1, b1, la, v, a2, b2, lb, g, source, target):
     def rows(latent, left, right, logw, pot):
-        return [
-            (0, latent[...]),
-            (LATENT, left[...]),
-            (ROW_LOGW, logw[...]),
-            (ROW_POT, pot),
-            (ROW_POT + 1, jnp.zeros((ROW_RIGHT - ROW_POT - 1, LANES), f32)),
-            (ROW_RIGHT, right[...]),
-            (ROW_RIGHT + RANK, jnp.zeros((PACK - ROW_RIGHT - RANK, LANES), f32)),
-        ]
-
-    for at, x in rows(v, a2, b2, lb, g[...]):
-        target[at : at + x.shape[0], :] = x
-    for at, x in rows(u, a1, b1, la, jnp.zeros((1, LANES), f32)):
-        for k in range(n):
-            source[k, at : at + x.shape[0], :] = x
+        zero = jnp.zeros((ROW_RIGHT - ROW_POT - 1, LANES), f32)
+        fill = jnp.zeros((PACK - ROW_RIGHT - RANK, LANES), f32)
+        return jnp.concatenate([latent, left, logw, pot, zero, right, fill], axis=0)
+
+    target[...] = rows(v[...], a2[:, 0, :], b2[:, 0, :], lb[...], g[...])
+    x = rows(u[...], a1[...], b1[...], la[...], jnp.zeros((1, LANES), f32))
+    for k in range(n):
+        source[k] = x
 
 
 def old_kernel(n, blocks, sg, tg, moment, lse_out, lse_own, carried, xh, xl, rt, rc, lt, b2, s0, s1, ph, pl_, held):
@@ -169,8 +217,7 @@
         rt[FEAT : 2 * FEAT, tile(t)] = low
         rt[2 * FEAT : BIAS, tile(t)] = hi
         pot = SCALE * (tg[t, ROW_POT : ROW_POT + 1, :] - half_square(tg[t]))
-        more = extra(ONES | {3 + k: x for k, x in enumerate(three(pot))})
-        transpose_into(rc, t, jnp.concatenate([hi, low, hi, more], axis=0))
+        transpose_into(rc, t, jnp.concatenate([hi, low, hi, shifted(pot)], axis=0))
         right = jnp.concatenate([tg[t, ROW_RIGHT:PACK, :], jnp.zeros((RIGHT + ROW_RIGHT - PACK, LANES), f32)], axis=0)
         hi, low = split(right)
         b2[0:RIGHT, tile(t)] = hi
@@ -258,7 +305,7 @@
     return jnp.concatenate([jnp.zeros((LATENT, LANES), f32), x, jnp.zeros((LANES - LATENT - MOMENT, LANES), f32)], axis=0)
 
 
-def first_g_kernel(n, blocks, parts, f, xh, xl, rc, out, lc, lt, s0, s1, held):
+def first_g_kernel(n, blocks, parts, f, xh, xl, rc, out, lc, lt, s0, s1, tops, totals):
     moment = unpack_moment(jnp.sum(parts[...], axis=0))
     lh, ll = left_operand(xh[...], xl[...], moment)
     lt[0:FEAT, :] = lh
@@ -266,24 +313,37 @@
     lt[2 * FEAT : BIAS, :] = ll
     put_bias(lt, f[...])
     for t in range(blocks):
-        transpose_into(lc, t, jnp.concatenate([lt[0:BIAS, tile(t)], extra(ONES)], axis=0))
-    lse_rows(rc, lt, out, n, s0, s1, held)
-
-
-def potential(blocks, parts, gathered):
-    x = LOG2E * pick(gathered, ROW_LOGW, blocks) - combine(parts[...])
-    square = jnp.concatenate([half_square(gathered[t]) for t in range(blocks)], axis=0)
-    return x, x * (1.0 / SCALE) + square
-
-
-def half_kernel(n, blocks, parts, gathered, stream, fixed_in, out, pot_out, fixed, s0, s1, held):
-    x, pot_out[...] = potential(blocks, parts, gathered)
-    put_bias(fixed, x)
-    lse_rows(stream, fixed, out, n, s0, s1, held)
+        more = shifted(f[t : t + 1, :] + HEADROOM)
+        transpose_into(lc, t, jnp.concatenate([lt[0:BIAS, tile(t)], more], axis=0))
+    lse_rows(rc, lt, out, n, s0, s1, tops, totals)
+
+
+def updated(blocks, parts, gathered):
+    return LOG2E * pick(gathered, ROW_LOGW, blocks) - combine(parts[...])
+
+
+def potential(blocks, x, gathered):
+    return x * (1.0 / SCALE) + jnp.concatenate([half_square(gathered[t]) for t in range(blocks)], axis=0)
+
+
+def half_kernel(n, blocks, parts, gathered, old, stream, fixed_in, other_in, out, x_out, fixed, other, *scratch):
+    x = updated(blocks, parts, gathered)
+    x_out[...] = x
+    put_bias(fixed, x, {3: 1.0, 4: 1.0, 5: 1.0})
+    for t in range(blocks):
+        restream(other, t, fixed, x[t : t + 1] + HEADROOM)
+    shifted_lse_rows(stream, fixed, old[...] + HEADROOM, out, n, *scratch)
+
+
+def last_half_kernel(n, blocks, parts, gathered, old, stream, fixed_in, out, pot_out, fixed, *scratch):
+    x = updated(blocks, parts, gathered)
+    pot_out[...] = potential(blocks, x, gathered)
+    put_bias(fixed, x, {3: 1.0, 4: 1.0, 5: 1.0})
+    shifted_lse_rows(stream, fixed, old[...] + HEADROOM, out, n, *scratch)
 
 
 def last_kernel(blocks, parts, gathered, pot_out):
-    _, pot_out[...] = potential(blocks, parts, gathered)
+    pot_out[...] = potential(blocks, updated(blocks, parts, gathered), gathered)
 
 
 def call(kernel, out, scratch=(), name=None, aliases={}):
@@ -306,13 +366,14 @@
 
 def shards(n_src, n_tgt, *args):
     (u, a1, b1, la, v, a2, b2, lb, g, old_moment) = args
-    v, a2, b2 = (x.reshape(-1, x.shape[-1]) for x in (v, a2, b2))
+    v = v.reshape(v.shape[2:])
+    a2, b2 = (x.transpose(3, 0, 1, 2).reshape(x.shape[3], 1, -1) for x in (a2, b2))
     flat = lambda x: x.reshape(1, -1)
     source, target = call(
         functools.partial(pack_kernel, n_tgt),
         [((n_tgt, PACK, LANES), f32), ((PACK, LANES), f32)],
         name="pack",
-    )(u.T, a1.T, b1.T, flat(la), v.T, a2.T, b2.T, flat(lb), flat(g))
+    )(u.T, a1.T, b1.T, flat(la), v.T, a2, b2, flat(lb), flat(g))
     sg = swap(source, "tgt")
     tg = lax.all_gather(target, "src", axis=0)
     bs, bt = n_tgt, n_src
@@ -349,7 +410,7 @@
     (moment,) = call(functools.partial(sum_kernel, n_src), [((n_src, 16, LANES), f32)], name="moment_sum")(
         swap(moment, "tgt")
     )
-    pipe = lambda cells, b: [((CHUNK, cells), f32), ((CHUNK, cells), f32), ((b, LANES), f32)]
+    pipe = lambda cells, b: [((CHUNK, cells), f32)] * 2 + [((b, LANES), f32)] * 2
     part, lc, lt = call(
         functools.partial(first_g_kernel, n_src, bs),
         [((n_src, bt, LANES), f32), ((rows, DEPTH), bf16), ((DEPTH, rows), bf16)],
@@ -358,14 +419,25 @@
     )(swap(moment, "src"), f, xh, xl, rc)
     half = lambda n, fixed, streamed, name: call(
         functools.partial(half_kernel, n, fixed),
-        [((n, streamed, LANES), f32), ((fixed, LANES), f32), ((DEPTH, fixed * LANES), bf16)],
+        [
+            ((n, streamed, LANES), f32),
+            ((fixed, LANES), f32),
+            ((DEPTH, fixed * LANES), bf16),
+            ((fixed * LANES, DEPTH), bf16),
+        ],
         pipe(fixed * LANES, streamed),
         name=name,
-        aliases={3: 2},
+        aliases={4: 2, 5: 3},
     )
-    part, _, rt = half(n_tgt, bt, bs, "first_f")(swap(part, "src"), tg, lc, rt)
-    part, _, lt = half(n_src, bs, bt, "second_g")(swap(part, "tgt"), sg, rc, lt)
-    part, g, rt = half(n_tgt, bt, bs, "second_f")(swap(part, "src"), tg, lc, rt)
+    part, g, rt, rc = half(n_tgt, bt, bs, "first_f")(swap(part, "src"), tg, f, lc, rt, rc)
+    part, f, lt, lc = half(n_src, bs, bt, "second_g")(swap(part, "tgt"), sg, g, rc, lt, lc)
+    part, g, _ = call(
+        functools.partial(last_half_kernel, n_tgt, bt),
+        [((n_tgt, bs, LANES), f32), ((bt, LANES), f32), ((DEPTH, cols), bf16)],
+        pipe(cols, bs),
+        name="second_f",
+        aliases={4: 2},
+    )(swap(part, "src"), tg, f, lc, rt)
     (f,) = call(functools.partial(last_kernel, bs), [((bs, LANES), f32)], name="last_f")(swap(part, "tgt"), sg)
     return f.reshape(-1), g.reshape(-1)
 

time: 147 us -> 150 us (1.020); the launches traced: 145 us -> 150 us
  blocking collectives: 105 us -> 111 us
  Pallas kernels: 30.1 us -> 24.8 us
  local copies, waits for them, and re-layouts: 1.53 us -> 6.36 us
    all_to_all x7, blocking collectives: 82.6 us -> 88.5 us  [swap(): return lax.all_to_all(x, axis, 0, 0)]
    unnamed x16 -> x20, local copies, waits for them, and re-layouts: 0.7 us -> 6.29 us
    pallas_call x9, Pallas kernels: 30.1 us -> 24.8 us  [call(): pl.pallas_call(kernel, out_shape=[jax.ShapeDtypeStruct(s, d) for s, d in...]
where the time goes in v3:
time: 150 us
  blocking collectives  111 us (74%)
  Pallas kernels  24.8 us (17%)
  starting transfers between devices  7.61 us (5%)
  local copies, waits for them, and re-layouts  6.36 us (4%)
    all_to_all x7, blocking collectives, swap(): return lax.all_to_all(x, axis, 0, 0)  88.5 us
    pallas_call x9, Pallas kernels, call(): pl.pallas_call(kernel, out_shape=[jax.ShapeDtypeStruct(s, d) for s, d in...  24.8 us
    all_gather x1, blocking collectives, shards(): tg = lax.all_gather(target, 'src', axis=0)  22.5 us
    all_to_all x1, starting transfers between devices, swap(): return lax.all_to_all(x, axis, 0, 0)  7.61 us
    unnamed x20, local copies, waits for them, and re-layouts  6.29 us
  transfers between devices with their start and end apart: 1, of which 0 were waited for; matrix products, arithmetic and copies ran while one was open for 0% of the time, Pallas kernels for 0%

profile of v3, /device:TPU:2, one launch (start us, length us, event | category | flops | bytes accessed | tf_op | source)
XLA Modules:
  0.0 150.5 jit_solution(10434372478435756674)
XLA Ops:
  0.6 0.7 copy-done.2
  1.4 0.7 copy-done
  2.1 0.7 copy-done.1
  2.8 0.7 copy-done.3
  3.5 0.7 copy-done.4
  4.3 0.7 copy-done.5
  5.6 0.7 copy-done.7
  6.3 0.7 copy-done.8
  6.9 1.0 pack.1
  7.9 7.6 %all-to-all-start = ((f32[16,112,128]{2,1,0:T(8,128)}), f32[16,112,128]{2,1,0:T(8,128)S(1)}, u32[]{:S(2)}, u32[]{:S(2)}) async-start(f32[16,112,128]{2,1,0:T(8,128)} %get-tuple-element.25), calls=%async_computation | async-start | bytes 1835008 | tf_op jit(solution)/shard_map/all_to_all | solution.py:364
  15.6 22.5 %all-gather = f32[1792,128]{1,0:T(8,128)S(1)} all-gather(f32[112,128]{1,0:T(8,128)S(1)} %get-tuple-element.26), channel_id=2, replica_groups=mesh['src'=16,'tgt'=16] {'src'}, dimensions={0}, use_global_device_ids=true | all-gather | bytes 974848 | tf_op jit(solution)/shard_map/all_gather | solution.py:378
  38.1 8.2 %old_plan.1 = (f32[16,16,128]{2,1,0:T(8,128)S(1)}, f32[16,128]{1,0:T(8,128)S(1)}, f32[48,2048]{1,0:T(8,128)S(1)}, bf16[80,2048]{1,0:T(8,128)(2,1)S(1)}, bf16[80,...) custom-call(f32[16,112,128]{2,1,0:T(8,128)S(1)} %all-to-all-done.sg.gathered, ...), custom_call_target="tpu_custom_call" | custom-call | tf_op jit(solution)/shard_map/old_plan/pallas_call | solution.py:351
  46.3 13.6 %all_to_all.40.parts = f32[16,16,128]{2,1,0:T(8,128)S(1)} all-to-all(f32[16,16,128]{2,1,0:T(8,128)S(1)} %get-tuple-element.27), channel_id=1, replica_groups=mesh['src'=16,'tgt'=16] {'tgt'}, dimensions={0} | all-to-all | bytes 262144 | tf_op jit(solution)/shard_map/all_to_all | solution.py:364
  60.4 11.1 %all_to_all.41.parts = f32[16,16,128]{2,1,0:T(8,128)S(1)} all-to-all(f32[16,16,128]{2,1,0:T(8,128)S(1)} %get-tuple-element.30), channel_id=1, replica_groups=mesh['src'=16,'tgt'=16] {'tgt'}, dimensions={0} | all-to-all | bytes 262144 | tf_op jit(solution)/shard_map/all_to_all | solution.py:364
  71.5 12.3 %all_to_all.42.parts = f32[16,16,128]{2,1,0:T(8,128)S(1)} all-to-all(f32[16,16,128]{2,1,0:T(8,128)S(1)} %moment_sum.1), channel_id=1, replica_groups=mesh['src'=16,'tgt'=16] {'src'}, dimensions={0} | all-to-all | bytes 262144 | tf_op jit(solution)/shard_map/all_to_all | solution.py:364
  83.8 4.7 %first_g.1 = (f32[16,16,128]{2,1,0:T(8,128)S(1)}, bf16[2048,256]{1,0:T(8,128)(2,1)S(1)}, bf16[256,2048]{1,0:T(8,128)(2,1)S(1)}) custom-call(f32[16,16,128]{2,1,0:T(8,128)S(1)} %all_to_all.42.parts, f32[16,128]{1,0:T(8,128)S(1)} %get-tuple-element.31.f.old, bf16[80,2048]{1,0:T(8,128)(2,1)S(1)} %get-tuple-element.32.xh, ...), custom_call_target="tpu_custom_call" | custom-call | tf_op jit(solution)/shard_map/first_g/pallas_call | solution.py:351
  88.4 11.7 %all_to_all.43.parts = f32[16,16,128]{2,1,0:T(8,128)S(1)} all-to-all(f32[16,16,128]{2,1,0:T(8,128)S(1)} %get-tuple-element.35), channel_id=1, replica_groups=mesh['src'=16,'tgt'=16] {'src'}, dimensions={0} | all-to-all | bytes 262144 | tf_op jit(solution)/shard_map/all_to_all | solution.py:364
  100.1 3.2 %first_f.1 = (f32[16,16,128]{2,1,0:T(8,128)S(1)}, f32[16,128]{1,0:T(8,128)S(1)}, bf16[256,2048]{1,0:T(8,128)(2,1)S(1)}, bf16[2048,256]{1,0:T(8,128)(2,1)S(1)}) custom-call(f32[16,16,128]{2,1,0:T(8,128)S(1)} %all_to_all.43.parts, f32[16,112,128]{2,1,0:T(8,128)S(1)} %bitcast.23, ...), custom_call_target="tpu_custom_call", output_to_operand_aliasing={{2}: (4, {}), {3}: (5, {})} | custom-call | tf_op jit(solution)/shard_map/first_f/pallas_call | solution.py:351
  103.3 11.1 %all_to_all.44.parts = f32[16,16,128]{2,1,0:T(8,128)S(1)} all-to-all(f32[16,16,128]{2,1,0:T(8,128)S(1)} %get-tuple-element.38), channel_id=1, replica_groups=mesh['src'=16,'tgt'=16] {'tgt'}, dimensions={0} | all-to-all | bytes 262144 | tf_op jit(solution)/shard_map/all_to_all | solution.py:364
  114.4 3.2 %second_g.1 = (f32[16,16,128]{2,1,0:T(8,128)S(1)}, f32[16,128]{1,0:T(8,128)S(1)}, bf16[256,2048]{1,0:T(8,128)(2,1)S(1)}, bf16[2048,256]{1,0:T(8,128)(2,1)S(1)}) custom-call(f32[16,16,128]{2,1,0:T(8,128)S(1)} %all_to_all.44.parts, f32[16,112,128]{2,1,0:T(8,128)S(1)} %all-to-all-done.sg.gathered, ...), custom_call_target="tpu_custom_call", output_to_operand_aliasing={{2}: (4, {}), {3}: (5, {})} | custom-call | tf_op jit(solution)/shard_map/second_g/pallas_call | solution.py:351
  117.6 11.5 %all_to_all.45.parts = f32[16,16,128]{2,1,0:T(8,128)S(1)} all-to-all(f32[16,16,128]{2,1,0:T(8,128)S(1)} %get-tuple-element.42), channel_id=1, replica_groups=mesh['src'=16,'tgt'=16] {'src'}, dimensions={0} | all-to-all | bytes 262144 | tf_op jit(solution)/shard_map/all_to_all | solution.py:364
  129.2 3.4 %second_f.1 = (f32[16,16,128]{2,1,0:T(8,128)S(1)}, f32[16,128]{1,0:T(8,128)}, bf16[256,2048]{1,0:T(8,128)(2,1)S(1)}) custom-call(f32[16,16,128]{2,1,0:T(8,128)S(1)} %all_to_all.45.parts, f32[16,112,128]{2,1,0:T(8,128)S(1)} %bitcast.24, f32[16,128]{1,0:T(8,128)S(1)} %get-tuple-element.43.old, ...), custom_call_target="tpu_custom_call", output_to_operand_aliasing={{2}: (4, {})} | custom-call | tf_op jit(solution)/shard_map/second_f/pallas_call | solution.py:351
  132.6 17.2 %all_to_all.46.parts = f32[16,16,128]{2,1,0:T(8,128)S(1)} all-to-all(f32[16,16,128]{2,1,0:T(8,128)S(1)} %get-tuple-element.46), channel_id=1, replica_groups=mesh['src'=16,'tgt'=16] {'tgt'}, dimensions={0} | all-to-all | bytes 262144 | tf_op jit(solution)/shard_map/all_to_all | solution.py:364
  149.8 0.7 last_f.1
  (16 shorter events, 1.2 us)
Async XLA Ops:
  0.6 0.7 copy-start.2
  1.4 0.7 copy-start
  2.1 0.7 copy-start.1
  2.8 0.7 copy-start.3
  3.5 0.7 copy-start.4
  4.2 0.7 copy-start.5
  5.0 0.7 copy-start.6
  5.6 0.7 copy-start.7
  6.3 0.7 copy-start.8
  7.9 7.6 %copy-start.9 = (f32[34,34]{1,0:T(8,128)S(1)}, f32[34,34]{1,0:T(8,128)}, u32[]{:S(2)}) copy-start(f32[34,34]{1,0:T(8,128)} %param.19) | copy-start | bytes 13876
  7.9 30.2 %all-to-all-start = ((f32[16,112,128]{2,1,0:T(8,128)}), f32[16,112,128]{2,1,0:T(8,128)S(1)}, u32[]{:S(2)}, u32[]{:S(2)}) async-start(f32[16,112,128]{2,1,0:T(8,128)} %get-tuple-element.25), calls=%async_computation | async-start | bytes 1835008 | tf_op jit(solution)/shard_map/all_to_all | solution.py:364

commit v4 on v3

--- a/solution.py
+++ b/solution.py
@@ -155,19 +155,26 @@
             reduce(b * (CHUNK // LANES) + k, s[b % 2], k * LANES)
 
 
-def lse_rows(stream, fixed, out_ref, n, s0, s1, tops, totals):
+def lse_rows(stream, fixed, out_ref, own_ref, s0, s1, tops, totals):
     mask = eye()
 
     def reduce(t, s, row):
         tops[t : t + 1, :], totals[t : t + 1, :] = reduce_rows(s, row, mask)
 
     pipeline(stream, fixed, s0, s1, reduce)
-    lse = tops[...] + jnp.log2(totals[...])
-    for k in range(n):
-        out_ref[k] = lse
-
-
-def shifted_lse_rows(stream, fixed, shift, out_ref, n, s0, s1, tops, totals):
+    write(tops[...] + jnp.log2(totals[...]), out_ref, own_ref)
+
+
+def write(x, *refs):
+    for ref in refs:
+        if len(ref.shape) == 2:
+            ref[...] = x
+        else:
+            for k in range(ref.shape[0]):
+                ref[k] = x
+
+
+def shifted_lse_rows(stream, fixed, shift, s0, s1, tops, totals, *refs):
     mask = eye()
 
     def reduce(t, s, row):
@@ -176,21 +183,24 @@
     pipeline(stream, fixed, s0, s1, reduce)
     total = totals[...]
     tops[...] = jnp.log2(total)
-    good = jnp.all((total >= SMALLEST) & (total <= LARGEST))
-
-    @pl.when(jnp.logical_not(good))
+
+    def good(total):
+        return jnp.all((total >= SMALLEST) & (total <= LARGEST))
+
+    @pl.when(jnp.logical_not(good(total)))
     def _():
         def step(t, carry):
-            s0[0:LANES, :] = dot(stream[pl.ds(pl.multiple_of(t * LANES, LANES), LANES), :], fixed[...])
-            top, total = reduce_rows(s0, 0, mask)
-            tops[pl.ds(t, 1), :] = top + jnp.log2(total)
+            @pl.when(jnp.logical_not(good(totals[pl.ds(t, 1), :])))
+            def _():
+                s0[0:LANES, :] = dot(stream[pl.ds(pl.multiple_of(t * LANES, LANES), LANES), :], fixed[...])
+                top, total = reduce_rows(s0, 0, mask)
+                tops[pl.ds(t, 1), :] = top + jnp.log2(total)
+
             return carry
 
         lax.fori_loop(0, stream.shape[0] // LANES, step, 0)
 
-    lse = tops[...] - shift
-    for k in range(n):
-        out_ref[k] = lse
+    write(tops[...] - shift, *refs)
 
 
 def combine(parts):
@@ -198,16 +208,24 @@
     return top + jnp.log2(jnp.sum(jnp.exp2(parts - top[None]), axis=0))
 
 
-def pack_kernel(n, u, a1, b1, la, v, a2, b2, lb, g, source, target):
+def pack_kernel(n, *refs):
+    (source, target), held, sems = refs[9:11], refs[11:20], refs[20]
+    copies = [pltpu.make_async_copy(refs[k], held[k], sems.at[k]) for k in range(9)]
+    for copy in copies:
+        copy.start()
+    for copy in copies:
+        copy.wait()
+    u, a1, b1, la, v, a2, b2, lb, g = held
+
     def rows(latent, left, right, logw, pot):
         zero = jnp.zeros((ROW_RIGHT - ROW_POT - 1, LANES), f32)
         fill = jnp.zeros((PACK - ROW_RIGHT - RANK, LANES), f32)
         return jnp.concatenate([latent, left, logw, pot, zero, right, fill], axis=0)
 
-    target[...] = rows(v[...], a2[:, 0, :], b2[:, 0, :], lb[...], g[...])
     x = rows(u[...], a1[...], b1[...], la[...], jnp.zeros((1, LANES), f32))
     for k in range(n):
         source[k] = x
+    target[...] = rows(v[...], a2[:, 0, :], b2[:, 0, :], lb[...], g[...])
 
 
 def old_kernel(n, blocks, sg, tg, moment, lse_out, lse_own, carried, xh, xl, rt, rc, lt, b2, s0, s1, ph, pl_, held):
@@ -305,7 +323,7 @@
     return jnp.concatenate([jnp.zeros((LATENT, LANES), f32), x, jnp.zeros((LANES - LATENT - MOMENT, LANES), f32)], axis=0)
 
 
-def first_g_kernel(n, blocks, parts, f, xh, xl, rc, out, lc, lt, s0, s1, tops, totals):
+def first_g_kernel(blocks, parts, f, xh, xl, rc, out, own, lc, lt, *scratch):
     moment = unpack_moment(jnp.sum(parts[...], axis=0))
     lh, ll = left_operand(xh[...], xl[...], moment)
     lt[0:FEAT, :] = lh
@@ -315,7 +333,7 @@
     for t in range(blocks):
         more = shifted(f[t : t + 1, :] + HEADROOM)
         transpose_into(lc, t, jnp.concatenate([lt[0:BIAS, tile(t)], more], axis=0))
-    lse_rows(rc, lt, out, n, s0, s1, tops, totals)
+    lse_rows(rc, lt, out, own, *scratch)
 
 
 def updated(blocks, parts, gathered):
@@ -326,36 +344,35 @@
     return x * (1.0 / SCALE) + jnp.concatenate([half_square(gathered[t]) for t in range(blocks)], axis=0)
 
 
-def half_kernel(n, blocks, parts, gathered, old, stream, fixed_in, other_in, out, x_out, fixed, other, *scratch):
+def half_kernel(blocks, as_shift, parts, gathered, shift, last, stream, fixed_in, other_in, out, own, fixed, other, *scratch):
     x = updated(blocks, parts, gathered)
-    x_out[...] = x
     put_bias(fixed, x, {3: 1.0, 4: 1.0, 5: 1.0})
     for t in range(blocks):
-        restream(other, t, fixed, x[t : t + 1] + HEADROOM)
-    shifted_lse_rows(stream, fixed, old[...] + HEADROOM, out, n, *scratch)
-
-
-def last_half_kernel(n, blocks, parts, gathered, old, stream, fixed_in, out, pot_out, fixed, *scratch):
+        restream(other, t, fixed, -last[t : t + 1, :])
+    shifted_lse_rows(stream, fixed, as_shift(shift[...]), *scratch, out, own)
+
+
+def last_half_kernel(blocks, parts, gathered, shift, stream, fixed_in, out, pot_out, fixed, *scratch):
     x = updated(blocks, parts, gathered)
     pot_out[...] = potential(blocks, x, gathered)
     put_bias(fixed, x, {3: 1.0, 4: 1.0, 5: 1.0})
-    shifted_lse_rows(stream, fixed, old[...] + HEADROOM, out, n, *scratch)
+    shifted_lse_rows(stream, fixed, -shift[...], *scratch, out)
 
 
 def last_kernel(blocks, parts, gathered, pot_out):
     pot_out[...] = potential(blocks, updated(blocks, parts, gathered), gathered)
 
 
-def call(kernel, out, scratch=(), name=None, aliases={}):
+def call(kernel, out, scratch=(), name=None, aliases={}, space=pltpu.VMEM, semaphores=[], vmem=32):
     spec = pl.BlockSpec(memory_space=pltpu.VMEM)
     return lambda *args: pl.pallas_call(
         kernel,
         out_shape=[jax.ShapeDtypeStruct(s, d) for s, d in out],
-        in_specs=[spec] * len(args),
+        in_specs=[pl.BlockSpec(memory_space=space)] * len(args),
         out_specs=[spec] * len(out),
-        scratch_shapes=[pltpu.VMEM(s, d) for s, d in scratch],
+        scratch_shapes=[pltpu.VMEM(s, d) for s, d in scratch] + semaphores,
         input_output_aliases=aliases,
-        compiler_params=pltpu.CompilerParams(vmem_limit_bytes=32 * 1024 * 1024),
+        compiler_params=pltpu.CompilerParams(vmem_limit_bytes=vmem * 1024 * 1024),
         name=name,
     )(*args)
 
@@ -369,11 +386,16 @@
     v = v.reshape(v.shape[2:])
     a2, b2 = (x.transpose(3, 0, 1, 2).reshape(x.shape[3], 1, -1) for x in (a2, b2))
     flat = lambda x: x.reshape(1, -1)
+    cells = (u.T, a1.T, b1.T, flat(la), v.T, a2, b2, flat(lb), flat(g))
     source, target = call(
         functools.partial(pack_kernel, n_tgt),
         [((n_tgt, PACK, LANES), f32), ((PACK, LANES), f32)],
+        [(x.shape, f32) for x in cells],
         name="pack",
-    )(u.T, a1.T, b1.T, flat(la), v.T, a2, b2, flat(lb), flat(g))
+        space=pltpu.HBM,
+        semaphores=[pltpu.SemaphoreType.DMA((len(cells),))],
+        vmem=63,
+    )(*cells)
     sg = swap(source, "tgt")
     tg = lax.all_gather(target, "src", axis=0)
     bs, bt = n_tgt, n_src
@@ -411,33 +433,37 @@
         swap(moment, "tgt")
     )
     pipe = lambda cells, b: [((CHUNK, cells), f32)] * 2 + [((b, LANES), f32)] * 2
-    part, lc, lt = call(
-        functools.partial(first_g_kernel, n_src, bs),
-        [((n_src, bt, LANES), f32), ((rows, DEPTH), bf16), ((DEPTH, rows), bf16)],
+    part, last_g, lc, lt = call(
+        functools.partial(first_g_kernel, bs),
+        [((n_src, bt, LANES), f32), ((bt, LANES), f32), ((rows, DEPTH), bf16), ((DEPTH, rows), bf16)],
         pipe(rows, bt),
         name="first_g",
     )(swap(moment, "src"), f, xh, xl, rc)
-    half = lambda n, fixed, streamed, name: call(
-        functools.partial(half_kernel, n, fixed),
+    half = lambda n, fixed, streamed, as_shift, name: call(
+        functools.partial(half_kernel, fixed, as_shift),
         [
             ((n, streamed, LANES), f32),
-            ((fixed, LANES), f32),
+            ((streamed, LANES), f32),
             ((DEPTH, fixed * LANES), bf16),
             ((fixed * LANES, DEPTH), bf16),
         ],
         pipe(fixed * LANES, streamed),
         name=name,
-        aliases={4: 2, 5: 3},
+        aliases={5: 2, 6: 3},
     )
-    part, g, rt, rc = half(n_tgt, bt, bs, "first_f")(swap(part, "src"), tg, f, lc, rt, rc)
-    part, f, lt, lc = half(n_src, bs, bt, "second_g")(swap(part, "tgt"), sg, g, rc, lt, lc)
+    part, last_f, rt, rc = half(n_tgt, bt, bs, lambda x: x + HEADROOM, "first_f")(
+        swap(part, "src"), tg, f, last_g, lc, rt, rc
+    )
+    part, _, lt, lc = half(n_src, bs, bt, lambda x: -x, "second_g")(
+        swap(part, "tgt"), sg, last_g, last_f, rc, lt, lc
+    )
     part, g, _ = call(
-        functools.partial(last_half_kernel, n_tgt, bt),
+        functools.partial(last_half_kernel, bt),
         [((n_tgt, bs, LANES), f32), ((bt, LANES), f32), ((DEPTH, cols), bf16)],
         pipe(cols, bs),
         name="second_f",
         aliases={4: 2},
-    )(swap(part, "src"), tg, f, lc, rt)
+    )(swap(part, "src"), tg, last_f, lc, rt)
     (f,) = call(functools.partial(last_kernel, bs), [((bs, LANES), f32)], name="last_f")(swap(part, "tgt"), sg)
     return f.reshape(-1), g.reshape(-1)
 

time: 150 us -> 144 us (0.960); the launches traced: 150 us -> 142 us
  blocking collectives: 111 us -> 105 us
  local copies, waits for them, and re-layouts: 6.36 us -> 0.82 us
  Pallas kernels: 24.8 us -> 28.1 us
    all_to_all x7, blocking collectives: 88.5 us -> 82.6 us  [swap(): return lax.all_to_all(x, axis, 0, 0)]
    unnamed x20 -> x4, local copies, waits for them, and re-layouts: 6.29 us -> 0.74 us
    pallas_call x9, Pallas kernels: 24.8 us -> 28.1 us  [call(): pl.pallas_call(kernel, out_shape=[jax.ShapeDtypeStruct(s, d) for s, d in...]
where the time goes in v4:
time: 144 us; the launch traced here: 142 us
  blocking collectives  105 us (73%)
  Pallas kernels  28.1 us (20%)
  starting transfers between devices  7.49 us (5%)
    all_to_all x7, blocking collectives, swap(): return lax.all_to_all(x, axis, 0, 0)  82.6 us
    pallas_call x9, Pallas kernels, call(): pl.pallas_call(kernel, out_shape=[jax.ShapeDtypeStruct(s, d) for s, d in...  28.1 us
    all_gather x1, blocking collectives, shards(): tg = lax.all_gather(target, 'src', axis=0)  22.5 us
    all_to_all x1, starting transfers between devices, swap(): return lax.all_to_all(x, axis, 0, 0)  7.49 us
  transfers between devices with their start and end apart: 1, of which 0 were waited for; matrix products, arithmetic and copies ran while one was open for 0% of the time, Pallas kernels for 0%

profile of v4, /device:TPU:2, one launch (start us, length us, event | category | flops | bytes accessed | tf_op | source)
XLA Modules:
  0.0 142.2 jit_solution(7072871024248985809)
XLA Ops:
  0.6 1.9 %pack.1 = (f32[16,112,128]{2,1,0:T(8,128)}, f32[112,128]{1,0:T(8,128)}) custom-call(f32[32,128]{1,0:T(8,128)} %bitcast.29, f32[34,128]{1,0:T(8,128)} %bitcast.25, f32[34,128]{1,0:T(8,128)} %bitcast.26, f32[1,128]{1,0:T(1,128)} %bitcast.32, f32[32,128]{1,0:T(8,128)} %bitcast.30, f32[34,1,128]{2,1,0:T(1,128)} %bitcast.27, f32[34,1,128]{2,1,0:T(1,128)} %bitcast.28, ...), custom_call_target="tpu_custom_call" | custom-call | tf_op jit(solution)/shard_map/pack/pallas_call | solution.py:368
  2.6 0.0 copy-start.1
  2.6 7.5 %all-to-all-start = ((f32[16,112,128]{2,1,0:T(8,128)}), f32[16,112,128]{2,1,0:T(8,128)S(1)}, u32[]{:S(2)}, u32[]{:S(2)}) async-start(f32[16,112,128]{2,1,0:T(8,128)} %get-tuple-element.25), calls=%async_computation | async-start | bytes 1835008 | tf_op jit(solution)/shard_map/all_to_all | solution.py:381
  10.1 0.0 copy-done.1
  10.1 0.0 copy-start
  10.1 0.1 pad.4.moment
  10.1 0.7 copy-done
  10.9 22.5 %all-gather = f32[1792,128]{1,0:T(8,128)S(1)} all-gather(f32[112,128]{1,0:T(8,128)S(1)} %copy-done), channel_id=2, replica_groups=mesh['src'=16,'tgt'=16] {'src'}, dimensions={0}, use_global_device_ids=true | all-gather | bytes 974848 | tf_op jit(solution)/shard_map/all_gather | solution.py:400
  33.4 0.0 all-to-all-done.sg.gathered
  33.4 8.8 %old_plan.1 = (f32[16,16,128]{2,1,0:T(8,128)S(1)}, f32[16,128]{1,0:T(8,128)S(1)}, f32[48,2048]{1,0:T(8,128)S(1)}, bf16[80,2048]{1,0:T(8,128)(2,1)S(1)}, bf16[80,...) custom-call(f32[16,112,128]{2,1,0:T(8,128)S(1)} %all-to-all-done.sg.gathered, ...), custom_call_target="tpu_custom_call" | custom-call | tf_op jit(solution)/shard_map/old_plan/pallas_call | solution.py:368
  42.1 13.6 %all_to_all.40.parts = f32[16,16,128]{2,1,0:T(8,128)S(1)} all-to-all(f32[16,16,128]{2,1,0:T(8,128)S(1)} %get-tuple-element.27), channel_id=1, replica_groups=mesh['src'=16,'tgt'=16] {'tgt'}, dimensions={0} | all-to-all | bytes 262144 | tf_op jit(solution)/shard_map/all_to_all | solution.py:381
  55.8 0.4 moment.1
  56.2 11.1 %all_to_all.41.parts = f32[16,16,128]{2,1,0:T(8,128)S(1)} all-to-all(f32[16,16,128]{2,1,0:T(8,128)S(1)} %get-tuple-element.30), channel_id=1, replica_groups=mesh['src'=16,'tgt'=16] {'tgt'}, dimensions={0} | all-to-all | bytes 262144 | tf_op jit(solution)/shard_map/all_to_all | solution.py:381
  67.3 12.3 %all_to_all.42.parts = f32[16,16,128]{2,1,0:T(8,128)S(1)} all-to-all(f32[16,16,128]{2,1,0:T(8,128)S(1)} %moment_sum.1), channel_id=1, replica_groups=mesh['src'=16,'tgt'=16] {'src'}, dimensions={0} | all-to-all | bytes 262144 | tf_op jit(solution)/shard_map/all_to_all | solution.py:381
  79.6 5.0 %first_g.1 = (f32[16,16,128]{2,1,0:T(8,128)S(1)}, f32[16,128]{1,0:T(8,128)S(1)}, bf16[2048,256]{1,0:T(8,128)(2,1)S(1)}, bf16[256,2048]{1,0:T(8,128)(2,1)S(1)}) custom-call(f32[16,16,128]{2,1,0:T(8,128)S(1)} %all_to_all.42.parts, f32[16,128]{1,0:T(8,128)S(1)} %get-tuple-element.31.f.shift, bf16[80,2048]{1,0:T(8,128)(2,1)S(1)} %get-tuple-element.32.xh, ...), custom_call_target="tpu_custom_call" | custom-call | tf_op jit(solution)/shard_map/first_g/pallas_call | solution.py:368
  84.5 11.6 %all_to_all.43.parts = f32[16,16,128]{2,1,0:T(8,128)S(1)} all-to-all(f32[16,16,128]{2,1,0:T(8,128)S(1)} %get-tuple-element.35), channel_id=1, replica_groups=mesh['src'=16,'tgt'=16] {'src'}, dimensions={0} | all-to-all | bytes 262144 | tf_op jit(solution)/shard_map/all_to_all | solution.py:381
  96.1 3.7 %first_f.1 = (f32[16,16,128]{2,1,0:T(8,128)S(1)}, f32[16,128]{1,0:T(8,128)S(1)}, bf16[256,2048]{1,0:T(8,128)(2,1)S(1)}, bf16[2048,256]{1,0:T(8,128)(2,1)S(1)}) custom-call(f32[16,16,128]{2,1,0:T(8,128)S(1)} %all_to_all.43.parts, f32[16,112,128]{2,1,0:T(8,128)S(1)} %bitcast.23, ...), custom_call_target="tpu_custom_call", output_to_operand_aliasing={{2}: (5, {}), {3}: (6, {})} | custom-call | tf_op jit(solution)/shard_map/first_f/pallas_call | solution.py:368
  99.8 11.4 %all_to_all.44.parts = f32[16,16,128]{2,1,0:T(8,128)S(1)} all-to-all(f32[16,16,128]{2,1,0:T(8,128)S(1)} %get-tuple-element.39), channel_id=1, replica_groups=mesh['src'=16,'tgt'=16] {'tgt'}, dimensions={0} | all-to-all | bytes 262144 | tf_op jit(solution)/shard_map/all_to_all | solution.py:381
  111.1 4.0 %second_g.1 = (f32[16,16,128]{2,1,0:T(8,128)S(1)}, f32[16,128]{1,0:T(8,128)}, bf16[256,2048]{1,0:T(8,128)(2,1)S(1)}, bf16[2048,256]{1,0:T(8,128)(2,1)S(1)}) custom-call(f32[16,16,128]{2,1,0:T(8,128)S(1)} %all_to_all.44.parts, f32[16,112,128]{2,1,0:T(8,128)S(1)} %all-to-all-done.sg.gathered, ...), custom_call_target="tpu_custom_call", output_to_operand_aliasing={{2}: (5, {}), {3}: (6, {})} | custom-call | tf_op jit(solution)/shard_map/second_g/pallas_call | solution.py:368
  115.1 11.3 %all_to_all.45.parts = f32[16,16,128]{2,1,0:T(8,128)S(1)} all-to-all(f32[16,16,128]{2,1,0:T(8,128)S(1)} %get-tuple-element.43), channel_id=1, replica_groups=mesh['src'=16,'tgt'=16] {'src'}, dimensions={0} | all-to-all | bytes 262144 | tf_op jit(solution)/shard_map/all_to_all | solution.py:381
  126.4 3.7 %second_f.1 = (f32[16,16,128]{2,1,0:T(8,128)S(1)}, f32[16,128]{1,0:T(8,128)}, bf16[256,2048]{1,0:T(8,128)(2,1)S(1)}) custom-call(f32[16,16,128]{2,1,0:T(8,128)S(1)} %all_to_all.45.parts, f32[16,112,128]{2,1,0:T(8,128)S(1)} %bitcast.24, f32[16,128]{1,0:T(8,128)S(1)} %get-tuple-element.40.last.shift, ...), custom_call_target="tpu_custom_call", output_to_operand_aliasing={{2}: (4, {})} | custom-call | tf_op jit(solution)/shard_map/second_f/pallas_call | solution.py:368
  130.2 11.3 %all_to_all.46.parts = f32[16,16,128]{2,1,0:T(8,128)S(1)} all-to-all(f32[16,16,128]{2,1,0:T(8,128)S(1)} %get-tuple-element.46), channel_id=1, replica_groups=mesh['src'=16,'tgt'=16] {'tgt'}, dimensions={0} | all-to-all | bytes 262144 | tf_op jit(solution)/shard_map/all_to_all | solution.py:381
  141.5 0.7 last_f.1
  (1 shorter events, 0.0 us)
Async XLA Ops:
  2.6 7.5 %copy-start.1 = (f32[34,34]{1,0:T(8,128)S(1)}, f32[34,34]{1,0:T(8,128)}, u32[]{:S(2)}) copy-start(f32[34,34]{1,0:T(8,128)} %param.19) | copy-start | bytes 13876
  2.6 30.8 %all-to-all-start = ((f32[16,112,128]{2,1,0:T(8,128)}), f32[16,112,128]{2,1,0:T(8,128)S(1)}, u32[]{:S(2)}, u32[]{:S(2)}) async-start(f32[16,112,128]{2,1,0:T(8,128)} %get-tuple-element.25), calls=%async_computation | async-start | bytes 1835008 | tf_op jit(solution)/shard_map/all_to_all | solution.py:381
  10.1 0.8 copy-start

commit v5 on v4

--- a/solution.py
+++ b/solution.py
@@ -237,6 +237,7 @@
         pot = SCALE * (tg[t, ROW_POT : ROW_POT + 1, :] - half_square(tg[t]))
         transpose_into(rc, t, jnp.concatenate([hi, low, hi, shifted(pot)], axis=0))
         right = jnp.concatenate([tg[t, ROW_RIGHT:PACK, :], jnp.zeros((RIGHT + ROW_RIGHT - PACK, LANES), f32)], axis=0)
+        right = jnp.where(iota(right.shape, 0) == RANK, 1.0, right)
         hi, low = split(right)
         b2[0:RIGHT, tile(t)] = hi
         b2[RIGHT:, tile(t)] = low
@@ -262,16 +263,13 @@
         for k in range(piece, cells, piece):
             top = jnp.maximum(top, s[k : k + piece, :])
         top = jnp.max(top, axis=0, keepdims=True)
-        total = jnp.zeros((piece, CHUNK), f32)
         for k in range(0, cells, piece):
-            p = jnp.exp2(s[k : k + piece, :] - top)
-            total = total + p
-            hi, low = split(p)
+            hi, low = split(jnp.exp2(s[k : k + piece, :] - top))
             ph[k : k + piece, :] = hi
             pl_[k : k + piece, :] = low
-        total = jnp.sum(total, axis=0, keepdims=True)
         c = dot(b2[...], ph[...])
         c = c[0:RIGHT] + c[RIGHT:] + dot(b2[0:RIGHT, :], pl_[...])
+        total = c[RANK : RANK + 1]
         carried[:, columns(b)] = c / total
         held[:, columns(b)] = top + jnp.log2(total)
 
@@ -344,23 +342,28 @@
     return x * (1.0 / SCALE) + jnp.concatenate([half_square(gathered[t]) for t in range(blocks)], axis=0)
 
 
-def half_kernel(blocks, as_shift, parts, gathered, shift, last, stream, fixed_in, other_in, out, own, fixed, other, *scratch):
-    x = updated(blocks, parts, gathered)
-    put_bias(fixed, x, {3: 1.0, 4: 1.0, 5: 1.0})
+def first_f_kernel(blocks, parts, gathered, f, last, stream, fixed_in, other_in, out, fixed, other, *scratch):
+    put_bias(fixed, updated(blocks, parts, gathered), {3: 1.0, 4: 1.0, 5: 1.0})
     for t in range(blocks):
         restream(other, t, fixed, -last[t : t + 1, :])
-    shifted_lse_rows(stream, fixed, as_shift(shift[...]), *scratch, out, own)
-
-
-def last_half_kernel(blocks, parts, gathered, shift, stream, fixed_in, out, pot_out, fixed, *scratch):
+    shifted_lse_rows(stream, fixed, f[...] + HEADROOM, *scratch, out)
+
+
+def second_g_kernel(blocks, parts, gathered, last, stream, fixed_in, out, fixed, *scratch):
+    put_bias(fixed, updated(blocks, parts, gathered), {3: 1.0, 4: 1.0, 5: 1.0})
+    shifted_lse_rows(stream, fixed, -last[...], *scratch, out)
+
+
+def second_f_kernel(blocks, parts, gathered, f, stream, fixed_in, out, x_out, fixed, *scratch):
     x = updated(blocks, parts, gathered)
-    pot_out[...] = potential(blocks, x, gathered)
+    x_out[...] = x
     put_bias(fixed, x, {3: 1.0, 4: 1.0, 5: 1.0})
-    shifted_lse_rows(stream, fixed, -shift[...], *scratch, out)
-
-
-def last_kernel(blocks, parts, gathered, pot_out):
-    pot_out[...] = potential(blocks, updated(blocks, parts, gathered), gathered)
+    shifted_lse_rows(stream, fixed, f[...] + HEADROOM, *scratch, out)
+
+
+def last_kernel(source_blocks, target_blocks, parts, sg, x, tg, f_out, g_out):
+    f_out[...] = potential(source_blocks, updated(source_blocks, parts, sg), sg)
+    g_out[...] = potential(target_blocks, x[...], tg)
 
 
 def call(kernel, out, scratch=(), name=None, aliases={}, space=pltpu.VMEM, semaphores=[], vmem=32):
@@ -439,32 +442,33 @@
         pipe(rows, bt),
         name="first_g",
     )(swap(moment, "src"), f, xh, xl, rc)
-    half = lambda n, fixed, streamed, as_shift, name: call(
-        functools.partial(half_kernel, fixed, as_shift),
-        [
-            ((n, streamed, LANES), f32),
-            ((streamed, LANES), f32),
-            ((DEPTH, fixed * LANES), bf16),
-            ((fixed * LANES, DEPTH), bf16),
-        ],
-        pipe(fixed * LANES, streamed),
-        name=name,
-        aliases={5: 2, 6: 3},
-    )
-    part, last_f, rt, rc = half(n_tgt, bt, bs, lambda x: x + HEADROOM, "first_f")(
-        swap(part, "src"), tg, f, last_g, lc, rt, rc
-    )
-    part, _, lt, lc = half(n_src, bs, bt, lambda x: -x, "second_g")(
-        swap(part, "tgt"), sg, last_g, last_f, rc, lt, lc
-    )
-    part, g, _ = call(
-        functools.partial(last_half_kernel, bt),
-        [((n_tgt, bs, LANES), f32), ((bt, LANES), f32), ((DEPTH, cols), bf16)],
+    fixed_t, fixed_s, stream_t = ((DEPTH, cols), bf16), ((DEPTH, rows), bf16), ((cols, DEPTH), bf16)
+    part, rt, rc = call(
+        functools.partial(first_f_kernel, bt),
+        [((n_tgt, bs, LANES), f32), fixed_t, stream_t],
+        pipe(cols, bs),
+        name="first_f",
+        aliases={5: 1, 6: 2},
+    )(swap(part, "src"), tg, f, last_g, lc, rt, rc)
+    part, _ = call(
+        functools.partial(second_g_kernel, bs),
+        [((n_src, bt, LANES), f32), fixed_s],
+        pipe(rows, bt),
+        name="second_g",
+        aliases={4: 1},
+    )(swap(part, "tgt"), sg, last_g, rc, lt)
+    part, x, _ = call(
+        functools.partial(second_f_kernel, bt),
+        [((n_tgt, bs, LANES), f32), ((bt, LANES), f32), fixed_t],
         pipe(cols, bs),
         name="second_f",
         aliases={4: 2},
-    )(swap(part, "src"), tg, last_f, lc, rt)
-    (f,) = call(functools.partial(last_kernel, bs), [((bs, LANES), f32)], name="last_f")(swap(part, "tgt"), sg)
+    )(swap(part, "src"), tg, f, lc, rt)
+    f, g = call(
+        functools.partial(last_kernel, bs, bt),
+        [((bs, LANES), f32), ((bt, LANES), f32)],
+        name="last",
+    )(swap(part, "tgt"), sg, x, tg)
     return f.reshape(-1), g.reshape(-1)
 
 

time: 144 us -> 140 us (0.972)
  Pallas kernels: 28.1 us -> 24.3 us
    pallas_call x9, Pallas kernels: 28.1 us -> 24.3 us  [call(): pl.pallas_call(kernel, out_shape=[jax.ShapeDtypeStruct(s, d) for s, d in...]
where the time goes in v5:
time: 140 us; the launch traced here: 138 us
  blocking collectives  105 us (75%)
  Pallas kernels  24.3 us (17%)
  starting transfers between devices  7.49 us (5%)
    all_to_all x7, blocking collectives, swap(): return lax.all_to_all(x, axis, 0, 0)  82.6 us
    pallas_call x9, Pallas kernels, call(): pl.pallas_call(kernel, out_shape=[jax.ShapeDtypeStruct(s, d) for s, d in...  24.3 us
    all_gather x1, blocking collectives, shards(): tg = lax.all_gather(target, 'src', axis=0)  22.5 us
    all_to_all x1, starting transfers between devices, swap(): return lax.all_to_all(x, axis, 0, 0)  7.49 us
  transfers between devices with their start and end apart: 1, of which 0 were waited for; matrix products, arithmetic and copies ran while one was open for 0% of the time, Pallas kernels for 0%

profile of v5, /device:TPU:2, one launch (start us, length us, event | category | flops | bytes accessed | tf_op | source)
XLA Modules:
  0.0 138.3 jit_solution(4745787006211412143)
XLA Ops:
  0.6 1.9 %pack.1 = (f32[16,112,128]{2,1,0:T(8,128)}, f32[112,128]{1,0:T(8,128)}) custom-call(f32[32,128]{1,0:T(8,128)} %bitcast.30, f32[34,128]{1,0:T(8,128)} %bitcast.26, f32[34,128]{1,0:T(8,128)} %bitcast.27, f32[1,128]{1,0:T(1,128)} %bitcast.32, f32[32,128]{1,0:T(8,128)} %bitcast.31, f32[34,1,128]{2,1,0:T(1,128)} %bitcast.28, f32[34,1,128]{2,1,0:T(1,128)} %bitcast.29, ...), custom_call_target="tpu_custom_call" | custom-call | tf_op jit(solution)/shard_map/pack/pallas_call | solution.py:371
  2.5 0.0 copy-start.1
  2.6 7.5 %all-to-all-start = ((f32[16,112,128]{2,1,0:T(8,128)}), f32[16,112,128]{2,1,0:T(8,128)S(1)}, u32[]{:S(2)}, u32[]{:S(2)}) async-start(f32[16,112,128]{2,1,0:T(8,128)} %get-tuple-element.25), calls=%async_computation | async-start | bytes 1835008 | tf_op jit(solution)/shard_map/all_to_all | solution.py:384
  10.1 0.0 copy-done.1
  10.1 0.0 copy-start
  10.1 0.1 pad.4.moment
  10.1 0.7 copy-done
  10.9 22.5 %all-gather = f32[1792,128]{1,0:T(8,128)S(1)} all-gather(f32[112,128]{1,0:T(8,128)S(1)} %copy-done), channel_id=2, replica_groups=mesh['src'=16,'tgt'=16] {'src'}, dimensions={0}, use_global_device_ids=true | all-gather | bytes 974848 | tf_op jit(solution)/shard_map/all_gather | solution.py:403
  33.3 0.0 all-to-all-done.sg.gathered
  33.4 7.4 %old_plan.1 = (f32[16,16,128]{2,1,0:T(8,128)S(1)}, f32[16,128]{1,0:T(8,128)S(1)}, f32[48,2048]{1,0:T(8,128)S(1)}, bf16[80,2048]{1,0:T(8,128)(2,1)S(1)}, bf16[80,...) custom-call(f32[16,112,128]{2,1,0:T(8,128)S(1)} %all-to-all-done.sg.gathered, ...), custom_call_target="tpu_custom_call" | custom-call | tf_op jit(solution)/shard_map/old_plan/pallas_call | solution.py:371
  40.8 13.7 %all_to_all.40.parts = f32[16,16,128]{2,1,0:T(8,128)S(1)} all-to-all(f32[16,16,128]{2,1,0:T(8,128)S(1)} %get-tuple-element.27), channel_id=1, replica_groups=mesh['src'=16,'tgt'=16] {'tgt'}, dimensions={0} | all-to-all | bytes 262144 | tf_op jit(solution)/shard_map/all_to_all | solution.py:384
  54.5 0.4 moment.1
  54.9 11.1 %all_to_all.41.parts = f32[16,16,128]{2,1,0:T(8,128)S(1)} all-to-all(f32[16,16,128]{2,1,0:T(8,128)S(1)} %get-tuple-element.30), channel_id=1, replica_groups=mesh['src'=16,'tgt'=16] {'tgt'}, dimensions={0} | all-to-all | bytes 262144 | tf_op jit(solution)/shard_map/all_to_all | solution.py:384
  66.0 12.3 %all_to_all.42.parts = f32[16,16,128]{2,1,0:T(8,128)S(1)} all-to-all(f32[16,16,128]{2,1,0:T(8,128)S(1)} %moment_sum.1), channel_id=1, replica_groups=mesh['src'=16,'tgt'=16] {'src'}, dimensions={0} | all-to-all | bytes 262144 | tf_op jit(solution)/shard_map/all_to_all | solution.py:384
  78.3 4.7 %first_g.1 = (f32[16,16,128]{2,1,0:T(8,128)S(1)}, f32[16,128]{1,0:T(8,128)S(1)}, bf16[2048,256]{1,0:T(8,128)(2,1)S(1)}, bf16[256,2048]{1,0:T(8,128)(2,1)S(1)}) custom-call(f32[16,16,128]{2,1,0:T(8,128)S(1)} %all_to_all.42.parts, f32[16,128]{1,0:T(8,128)S(1)} %get-tuple-element.31.f, bf16[80,2048]{1,0:T(8,128)(2,1)S(1)} %get-tuple-element.32.xh, ...), custom_call_target="tpu_custom_call" | custom-call | tf_op jit(solution)/shard_map/first_g/pallas_call | solution.py:371
  83.0 11.6 %all_to_all.43.parts = f32[16,16,128]{2,1,0:T(8,128)S(1)} all-to-all(f32[16,16,128]{2,1,0:T(8,128)S(1)} %get-tuple-element.35), channel_id=1, replica_groups=mesh['src'=16,'tgt'=16] {'src'}, dimensions={0} | all-to-all | bytes 262144 | tf_op jit(solution)/shard_map/all_to_all | solution.py:384
  94.5 3.4 %first_f.1 = (f32[16,16,128]{2,1,0:T(8,128)S(1)}, bf16[256,2048]{1,0:T(8,128)(2,1)S(1)}, bf16[2048,256]{1,0:T(8,128)(2,1)S(1)}) custom-call(f32[16,16,128]{2,1,0:T(8,128)S(1)} %all_to_all.43.parts, f32[16,112,128]{2,1,0:T(8,128)S(1)} %bitcast.23, f32[16,128]{1,0:T(8,128)S(1)} %get-tuple-element.31.f, ...), custom_call_target="tpu_custom_call", output_to_operand_aliasing={{1}: (5, {}), {2}: (6, {})} | custom-call | tf_op jit(solution)/shard_map/first_f/pallas_call | solution.py:371
  97.9 11.3 %all_to_all.44.parts = f32[16,16,128]{2,1,0:T(8,128)S(1)} all-to-all(f32[16,16,128]{2,1,0:T(8,128)S(1)} %get-tuple-element.39), channel_id=1, replica_groups=mesh['src'=16,'tgt'=16] {'tgt'}, dimensions={0} | all-to-all | bytes 262144 | tf_op jit(solution)/shard_map/all_to_all | solution.py:384
  109.3 2.8 %second_g.1 = (f32[16,16,128]{2,1,0:T(8,128)S(1)}, bf16[256,2048]{1,0:T(8,128)(2,1)S(1)}) custom-call(f32[16,16,128]{2,1,0:T(8,128)S(1)} %all_to_all.44.parts, f32[16,112,128]{2,1,0:T(8,128)S(1)} %all-to-all-done.sg.gathered, f32[16,128]{1,0:T(8,128)S(1)} %get-tuple-element.36.last, ...), custom_call_target="tpu_custom_call", output_to_operand_aliasing={{1}: (4, {})} | custom-call | tf_op jit(solution)/shard_map/second_g/pallas_call | solution.py:371
  112.1 11.3 %all_to_all.45.parts = f32[16,16,128]{2,1,0:T(8,128)S(1)} all-to-all(f32[16,16,128]{2,1,0:T(8,128)S(1)} %get-tuple-element.42), channel_id=1, replica_groups=mesh['src'=16,'tgt'=16] {'src'}, dimensions={0} | all-to-all | bytes 262144 | tf_op jit(solution)/shard_map/all_to_all | solution.py:384
  123.4 2.9 %second_f.1 = (f32[16,16,128]{2,1,0:T(8,128)S(1)}, f32[16,128]{1,0:T(8,128)S(1)}, bf16[256,2048]{1,0:T(8,128)(2,1)S(1)}) custom-call(f32[16,16,128]{2,1,0:T(8,128)S(1)} %all_to_all.45.parts, f32[16,112,128]{2,1,0:T(8,128)S(1)} %bitcast.24, f32[16,128]{1,0:T(8,128)S(1)} %get-tuple-element.31.f, ...), custom_call_target="tpu_custom_call", output_to_operand_aliasing={{2}: (4, {})} | custom-call | tf_op jit(solution)/shard_map/second_f/pallas_call | solution.py:371
  126.3 11.3 %all_to_all.46.parts = f32[16,16,128]{2,1,0:T(8,128)S(1)} all-to-all(f32[16,16,128]{2,1,0:T(8,128)S(1)} %get-tuple-element.44), channel_id=1, replica_groups=mesh['src'=16,'tgt'=16] {'tgt'}, dimensions={0} | all-to-all | bytes 262144 | tf_op jit(solution)/shard_map/all_to_all | solution.py:384
  137.6 0.7 last.1
  (1 shorter events, 0.0 us)
Async XLA Ops:
  2.5 7.5 %copy-start.1 = (f32[34,34]{1,0:T(8,128)S(1)}, f32[34,34]{1,0:T(8,128)}, u32[]{:S(2)}) copy-start(f32[34,34]{1,0:T(8,128)} %param.19) | copy-start | bytes 13876
  2.6 30.8 %all-to-all-start = ((f32[16,112,128]{2,1,0:T(8,128)}), f32[16,112,128]{2,1,0:T(8,128)S(1)}, u32[]{:S(2)}, u32[]{:S(2)}) async-start(f32[16,112,128]{2,1,0:T(8,128)} %get-tuple-element.25), calls=%async_computation | async-start | bytes 1835008 | tf_op jit(solution)/shard_map/all_to_all | solution.py:384
  10.1 0.8 copy-start

commit v6 on v5

--- a/solution.py
+++ b/solution.py
@@ -144,7 +144,7 @@
     return to_lanes(jnp.sum(jnp.concatenate(totals, axis=0), axis=1, keepdims=True), mask)
 
 
-def pipeline(stream, fixed, s0, s1, reduce):
+def pipeline(stream, fixed, s0, s1, reduce, beside):
     s = (s0, s1)
     steps = stream.shape[0] // CHUNK
     s0[...] = dot(stream[0:CHUNK, :], fixed[...])
@@ -152,16 +152,17 @@
         if b + 1 < steps:
             s[(b + 1) % 2][...] = dot(stream[(b + 1) * CHUNK : (b + 2) * CHUNK, :], fixed[...])
         for k in range(CHUNK // LANES):
+            beside(b * (CHUNK // LANES) + k)
             reduce(b * (CHUNK // LANES) + k, s[b % 2], k * LANES)
 
 
-def lse_rows(stream, fixed, out_ref, own_ref, s0, s1, tops, totals):
+def lse_rows(beside, stream, fixed, out_ref, own_ref, s0, s1, tops, totals):
     mask = eye()
 
     def reduce(t, s, row):
         tops[t : t + 1, :], totals[t : t + 1, :] = reduce_rows(s, row, mask)
 
-    pipeline(stream, fixed, s0, s1, reduce)
+    pipeline(stream, fixed, s0, s1, reduce, beside)
     write(tops[...] + jnp.log2(totals[...]), out_ref, own_ref)
 
 
@@ -174,13 +175,13 @@
                 ref[k] = x
 
 
-def shifted_lse_rows(stream, fixed, shift, s0, s1, tops, totals, *refs):
+def shifted_lse_rows(beside, stream, fixed, shift, s0, s1, tops, totals, *refs):
     mask = eye()
 
     def reduce(t, s, row):
         totals[t : t + 1, :] = add_rows(s, row, mask)
 
-    pipeline(stream, fixed, s0, s1, reduce)
+    pipeline(stream, fixed, s0, s1, reduce, beside)
     total = totals[...]
     tops[...] = jnp.log2(total)
 
@@ -203,6 +204,10 @@
     write(tops[...] - shift, *refs)
 
 
+def nothing(t):
+    pass
+
+
 def combine(parts):
     top = jnp.max(parts, axis=0)
     return top + jnp.log2(jnp.sum(jnp.exp2(parts - top[None]), axis=0))
@@ -228,7 +233,7 @@
     target[...] = rows(v[...], a2[:, 0, :], b2[:, 0, :], lb[...], g[...])
 
 
-def old_kernel(n, blocks, sg, tg, moment, lse_out, lse_own, carried, xh, xl, rt, rc, lt, b2, s0, s1, ph, pl_, held):
+def old_kernel(n, blocks, sg, tg, moment, lse_out, lse_own, carried, xh, xl, rt, rc, lt, b2, s0, s1, ph0, pl0, ph1, pl1, held):
     for t in range(blocks):
         hi, low = split(features(tg[t]))
         rt[0:FEAT, tile(t)] = hi
@@ -236,11 +241,6 @@
         rt[2 * FEAT : BIAS, tile(t)] = hi
         pot = SCALE * (tg[t, ROW_POT : ROW_POT + 1, :] - half_square(tg[t]))
         transpose_into(rc, t, jnp.concatenate([hi, low, hi, shifted(pot)], axis=0))
-        right = jnp.concatenate([tg[t, ROW_RIGHT:PACK, :], jnp.zeros((RIGHT + ROW_RIGHT - PACK, LANES), f32)], axis=0)
-        right = jnp.where(iota(right.shape, 0) == RANK, 1.0, right)
-        hi, low = split(right)
-        b2[0:RIGHT, tile(t)] = hi
-        b2[RIGHT:, tile(t)] = low
         hi, low = split(features(sg[t]))
         xh[:, tile(t)] = hi
         xl[:, tile(t)] = low
@@ -252,37 +252,44 @@
     cells, piece = rc.shape[0], 64
     steps = lt.shape[1] // CHUNK
 
+    s, p = (s0, s1), ((ph0, pl0), (ph1, pl1))
+
     def columns(b):
-        return pl.ds(pl.multiple_of(b * CHUNK, CHUNK), CHUNK)
-
-    def scores(b, s):
-        s[...] = dot(rc[...], lt[:, columns(b)])
-
-    def plan(b, s):
-        top = s[0:piece, :]
+        return slice(b * CHUNK, (b + 1) * CHUNK)
+
+    def scores(b):
+        s[b % 2][...] = dot(rc[...], lt[:, columns(b)])
+
+    def exponentials(b):
+        x, (high, rest) = s[b % 2], p[b % 2]
+        top = x[0:piece, :]
         for k in range(piece, cells, piece):
-            top = jnp.maximum(top, s[k : k + piece, :])
+            top = jnp.maximum(top, x[k : k + piece, :])
         top = jnp.max(top, axis=0, keepdims=True)
         for k in range(0, cells, piece):
-            hi, low = split(jnp.exp2(s[k : k + piece, :] - top))
-            ph[k : k + piece, :] = hi
-            pl_[k : k + piece, :] = low
-        c = dot(b2[...], ph[...])
-        c = c[0:RIGHT] + c[RIGHT:] + dot(b2[0:RIGHT, :], pl_[...])
+            high[k : k + piece, :], rest[k : k + piece, :] = split(jnp.exp2(x[k : k + piece, :] - top))
+        held[:, columns(b)] = top
+
+    def carry(b):
+        high, rest = p[b % 2]
+        c = dot(b2[...], high[...])
+        c = c[0:RIGHT] + c[RIGHT:] + dot(b2[0:RIGHT, :], rest[...])
         total = c[RANK : RANK + 1]
         carried[:, columns(b)] = c / total
-        held[:, columns(b)] = top + jnp.log2(total)
-
-    scores(0, s0)
-
-    def step(i, carry):
-        scores(2 * i + 1, s1)
-        plan(2 * i, s0)
-        scores(lax.rem(2 * i + 2, steps), s0)
-        plan(2 * i + 1, s1)
-        return carry
-
-    lax.fori_loop(0, steps // 2, step, 0)
+        held[:, columns(b)] = held[:, columns(b)] + jnp.log2(total)
+
+    scores(0)
+    for t in range(blocks):
+        right = jnp.concatenate([tg[t, ROW_RIGHT:PACK, :], jnp.zeros((RIGHT + ROW_RIGHT - PACK, LANES), f32)], axis=0)
+        right = jnp.where(iota(right.shape, 0) == RANK, 1.0, right)
+        b2[0:RIGHT, tile(t)], b2[RIGHT:, tile(t)] = split(right)
+    for b in range(steps):
+        if b + 1 < steps:
+            scores(b + 1)
+        exponentials(b)
+        if b:
+            carry(b - 1)
+    carry(steps - 1)
     lse = jnp.concatenate([held[:, tile(t)] for t in range(cells // LANES)], axis=0)
     lse_own[...] = lse
     for k in range(n):
@@ -328,10 +335,15 @@
     lt[FEAT : 2 * FEAT, :] = lh
     lt[2 * FEAT : BIAS, :] = ll
     put_bias(lt, f[...])
-    for t in range(blocks):
-        more = shifted(f[t : t + 1, :] + HEADROOM)
-        transpose_into(lc, t, jnp.concatenate([lt[0:BIAS, tile(t)], more], axis=0))
-    lse_rows(rc, lt, out, own, *scratch)
+
+    def transpose(t):
+        if t < blocks:
+            more = shifted(f[t : t + 1, :] + HEADROOM)
+            transpose_into(lc, t, jnp.concatenate([lt[0:BIAS, tile(t)], more], axis=0))
+
+    for t in range(rc.shape[0] // LANES, blocks):
+        transpose(t)
+    lse_rows(transpose, rc, lt, out, own, *scratch)
 
 
 def updated(blocks, parts, gathered):
@@ -344,21 +356,26 @@
 
 def first_f_kernel(blocks, parts, gathered, f, last, stream, fixed_in, other_in, out, fixed, other, *scratch):
     put_bias(fixed, updated(blocks, parts, gathered), {3: 1.0, 4: 1.0, 5: 1.0})
-    for t in range(blocks):
-        restream(other, t, fixed, -last[t : t + 1, :])
-    shifted_lse_rows(stream, fixed, f[...] + HEADROOM, *scratch, out)
+
+    def renew(t):
+        if t < blocks:
+            restream(other, t, fixed, -last[t : t + 1, :])
+
+    for t in range(stream.shape[0] // LANES, blocks):
+        renew(t)
+    shifted_lse_rows(renew, stream, fixed, f[...] + HEADROOM, *scratch, out)
 
 
 def second_g_kernel(blocks, parts, gathered, last, stream, fixed_in, out, fixed, *scratch):
     put_bias(fixed, updated(blocks, parts, gathered), {3: 1.0, 4: 1.0, 5: 1.0})
-    shifted_lse_rows(stream, fixed, -last[...], *scratch, out)
+    shifted_lse_rows(nothing, stream, fixed, -last[...], *scratch, out)
 
 
 def second_f_kernel(blocks, parts, gathered, f, stream, fixed_in, out, x_out, fixed, *scratch):
     x = updated(blocks, parts, gathered)
     x_out[...] = x
     put_bias(fixed, x, {3: 1.0, 4: 1.0, 5: 1.0})
-    shifted_lse_rows(stream, fixed, f[...] + HEADROOM, *scratch, out)
+    shifted_lse_rows(nothing, stream, fixed, f[...] + HEADROOM, *scratch, out)
 
 
 def last_kernel(source_blocks, target_blocks, parts, sg, x, tg, f_out, g_out):
@@ -421,6 +438,8 @@
             ((2 * RIGHT, cols), bf16),
             ((cols, CHUNK), f32),
             ((cols, CHUNK), f32),
+            ((cols, CHUNK), bf16),
+            ((cols, CHUNK), bf16),
             ((cols, CHUNK), bf16),
             ((cols, CHUNK), bf16),
             ((1, rows), f32),

time: 140 us -> 139 us (level)
  no operation moved by 1% of the time
where the time goes in v6:
time: 139 us; the launch traced here: 137 us
  blocking collectives  105 us (76%)
  Pallas kernels  23.2 us (17%)
  starting transfers between devices  7.49 us (5%)
    all_to_all x7, blocking collectives, swap(): return lax.all_to_all(x, axis, 0, 0)  82.6 us
    pallas_call x9, Pallas kernels, call(): pl.pallas_call(kernel, out_shape=[jax.ShapeDtypeStruct(s, d) for s, d in...  23.2 us
    all_gather x1, blocking collectives, shards(): tg = lax.all_gather(target, 'src', axis=0)  22.5 us
    all_to_all x1, starting transfers between devices, swap(): return lax.all_to_all(x, axis, 0, 0)  7.49 us
  transfers between devices with their start and end apart: 1, of which 0 were waited for; matrix products, arithmetic and copies ran while one was open for 0% of the time, Pallas kernels for 0%

profile of v6, /device:TPU:2, one launch (start us, length us, event | category | flops | bytes accessed | tf_op | source)
XLA Modules:
  0.0 137.2 jit_solution(17805928101862573236)
XLA Ops:
  0.6 1.9 %pack.1 = (f32[16,112,128]{2,1,0:T(8,128)}, f32[112,128]{1,0:T(8,128)}) custom-call(f32[32,128]{1,0:T(8,128)} %bitcast.30, f32[34,128]{1,0:T(8,128)} %bitcast.26, f32[34,128]{1,0:T(8,128)} %bitcast.27, f32[1,128]{1,0:T(1,128)} %bitcast.32, f32[32,128]{1,0:T(8,128)} %bitcast.31, f32[34,1,128]{2,1,0:T(1,128)} %bitcast.28, f32[34,1,128]{2,1,0:T(1,128)} %bitcast.29, ...), custom_call_target="tpu_custom_call" | custom-call | tf_op jit(solution)/shard_map/pack/pallas_call | solution.py:388
  2.5 0.0 copy-start.1
  2.6 7.5 %all-to-all-start = ((f32[16,112,128]{2,1,0:T(8,128)}), f32[16,112,128]{2,1,0:T(8,128)S(1)}, u32[]{:S(2)}, u32[]{:S(2)}) async-start(f32[16,112,128]{2,1,0:T(8,128)} %get-tuple-element.25), calls=%async_computation | async-start | bytes 1835008 | tf_op jit(solution)/shard_map/all_to_all | solution.py:401
  10.1 0.0 copy-done.1
  10.1 0.0 copy-start
  10.1 0.1 pad.4.moment
  10.1 0.7 copy-done
  10.9 22.5 %all-gather = f32[1792,128]{1,0:T(8,128)S(1)} all-gather(f32[112,128]{1,0:T(8,128)S(1)} %copy-done), channel_id=2, replica_groups=mesh['src'=16,'tgt'=16] {'src'}, dimensions={0}, use_global_device_ids=true | all-gather | bytes 974848 | tf_op jit(solution)/shard_map/all_gather | solution.py:420
  33.3 0.0 all-to-all-done.sg.gathered
  33.4 6.7 %old_plan.1 = (f32[16,16,128]{2,1,0:T(8,128)S(1)}, f32[16,128]{1,0:T(8,128)S(1)}, f32[48,2048]{1,0:T(8,128)S(1)}, bf16[80,2048]{1,0:T(8,128)(2,1)S(1)}, bf16[80,...) custom-call(f32[16,112,128]{2,1,0:T(8,128)S(1)} %all-to-all-done.sg.gathered, ...), custom_call_target="tpu_custom_call" | custom-call | tf_op jit(solution)/shard_map/old_plan/pallas_call | solution.py:388
  40.1 13.6 %all_to_all.40.parts = f32[16,16,128]{2,1,0:T(8,128)S(1)} all-to-all(f32[16,16,128]{2,1,0:T(8,128)S(1)} %get-tuple-element.27), channel_id=1, replica_groups=mesh['src'=16,'tgt'=16] {'tgt'}, dimensions={0} | all-to-all | bytes 262144 | tf_op jit(solution)/shard_map/all_to_all | solution.py:401
  53.7 0.4 moment.1
  54.1 11.1 %all_to_all.41.parts = f32[16,16,128]{2,1,0:T(8,128)S(1)} all-to-all(f32[16,16,128]{2,1,0:T(8,128)S(1)} %get-tuple-element.30), channel_id=1, replica_groups=mesh['src'=16,'tgt'=16] {'tgt'}, dimensions={0} | all-to-all | bytes 262144 | tf_op jit(solution)/shard_map/all_to_all | solution.py:401
  65.2 12.3 %all_to_all.42.parts = f32[16,16,128]{2,1,0:T(8,128)S(1)} all-to-all(f32[16,16,128]{2,1,0:T(8,128)S(1)} %moment_sum.1), channel_id=1, replica_groups=mesh['src'=16,'tgt'=16] {'src'}, dimensions={0} | all-to-all | bytes 262144 | tf_op jit(solution)/shard_map/all_to_all | solution.py:401
  77.5 4.5 %first_g.1 = (f32[16,16,128]{2,1,0:T(8,128)S(1)}, f32[16,128]{1,0:T(8,128)S(1)}, bf16[2048,256]{1,0:T(8,128)(2,1)S(1)}, bf16[256,2048]{1,0:T(8,128)(2,1)S(1)}) custom-call(f32[16,16,128]{2,1,0:T(8,128)S(1)} %all_to_all.42.parts, f32[16,128]{1,0:T(8,128)S(1)} %get-tuple-element.31.f, bf16[80,2048]{1,0:T(8,128)(2,1)S(1)} %get-tuple-element.32.xh, ...), custom_call_target="tpu_custom_call" | custom-call | tf_op jit(solution)/shard_map/first_g/pallas_call | solution.py:388
  82.0 11.6 %all_to_all.43.parts = f32[16,16,128]{2,1,0:T(8,128)S(1)} all-to-all(f32[16,16,128]{2,1,0:T(8,128)S(1)} %get-tuple-element.35), channel_id=1, replica_groups=mesh['src'=16,'tgt'=16] {'src'}, dimensions={0} | all-to-all | bytes 262144 | tf_op jit(solution)/shard_map/all_to_all | solution.py:401
  93.6 3.2 %first_f.1 = (f32[16,16,128]{2,1,0:T(8,128)S(1)}, bf16[256,2048]{1,0:T(8,128)(2,1)S(1)}, bf16[2048,256]{1,0:T(8,128)(2,1)S(1)}) custom-call(f32[16,16,128]{2,1,0:T(8,128)S(1)} %all_to_all.43.parts, f32[16,112,128]{2,1,0:T(8,128)S(1)} %bitcast.23, f32[16,128]{1,0:T(8,128)S(1)} %get-tuple-element.31.f, ...), custom_call_target="tpu_custom_call", output_to_operand_aliasing={{1}: (5, {}), {2}: (6, {})} | custom-call | tf_op jit(solution)/shard_map/first_f/pallas_call | solution.py:388
  96.8 11.3 %all_to_all.44.parts = f32[16,16,128]{2,1,0:T(8,128)S(1)} all-to-all(f32[16,16,128]{2,1,0:T(8,128)S(1)} %get-tuple-element.39), channel_id=1, replica_groups=mesh['src'=16,'tgt'=16] {'tgt'}, dimensions={0} | all-to-all | bytes 262144 | tf_op jit(solution)/shard_map/all_to_all | solution.py:401
  108.2 2.8 %second_g.1 = (f32[16,16,128]{2,1,0:T(8,128)S(1)}, bf16[256,2048]{1,0:T(8,128)(2,1)S(1)}) custom-call(f32[16,16,128]{2,1,0:T(8,128)S(1)} %all_to_all.44.parts, f32[16,112,128]{2,1,0:T(8,128)S(1)} %all-to-all-done.sg.gathered, f32[16,128]{1,0:T(8,128)S(1)} %get-tuple-element.36.last, ...), custom_call_target="tpu_custom_call", output_to_operand_aliasing={{1}: (4, {})} | custom-call | tf_op jit(solution)/shard_map/second_g/pallas_call | solution.py:388
  111.0 11.3 %all_to_all.45.parts = f32[16,16,128]{2,1,0:T(8,128)S(1)} all-to-all(f32[16,16,128]{2,1,0:T(8,128)S(1)} %get-tuple-element.42), channel_id=1, replica_groups=mesh['src'=16,'tgt'=16] {'src'}, dimensions={0} | all-to-all | bytes 262144 | tf_op jit(solution)/shard_map/all_to_all | solution.py:401
  122.3 2.9 %second_f.1 = (f32[16,16,128]{2,1,0:T(8,128)S(1)}, f32[16,128]{1,0:T(8,128)S(1)}, bf16[256,2048]{1,0:T(8,128)(2,1)S(1)}) custom-call(f32[16,16,128]{2,1,0:T(8,128)S(1)} %all_to_all.45.parts, f32[16,112,128]{2,1,0:T(8,128)S(1)} %bitcast.24, f32[16,128]{1,0:T(8,128)S(1)} %get-tuple-element.31.f, ...), custom_call_target="tpu_custom_call", output_to_operand_aliasing={{2}: (4, {})} | custom-call | tf_op jit(solution)/shard_map/second_f/pallas_call | solution.py:388
  125.2 11.3 %all_to_all.46.parts = f32[16,16,128]{2,1,0:T(8,128)S(1)} all-to-all(f32[16,16,128]{2,1,0:T(8,128)S(1)} %get-tuple-element.44), channel_id=1, replica_groups=mesh['src'=16,'tgt'=16] {'tgt'}, dimensions={0} | all-to-all | bytes 262144 | tf_op jit(solution)/shard_map/all_to_all | solution.py:401
  136.5 0.7 last.1
  (1 shorter events, 0.0 us)
Async XLA Ops:
  2.5 7.5 %copy-start.1 = (f32[34,34]{1,0:T(8,128)S(1)}, f32[34,34]{1,0:T(8,128)}, u32[]{:S(2)}) copy-start(f32[34,34]{1,0:T(8,128)} %param.19) | copy-start | bytes 13876
  2.6 30.8 %all-to-all-start = ((f32[16,112,128]{2,1,0:T(8,128)}), f32[16,112,128]{2,1,0:T(8,128)S(1)}, u32[]{:S(2)}, u32[]{:S(2)}) async-start(f32[16,112,128]{2,1,0:T(8,128)} %get-tuple-element.25), calls=%async_computation | async-start | bytes 1835008 | tf_op jit(solution)/shard_map/all_to_all | solution.py:401
  10.1 0.8 copy-start

commit v7 on v6

--- a/solution.py
+++ b/solution.py
@@ -233,7 +233,7 @@
     target[...] = rows(v[...], a2[:, 0, :], b2[:, 0, :], lb[...], g[...])
 
 
-def old_kernel(n, blocks, sg, tg, moment, lse_out, lse_own, carried, xh, xl, rt, rc, lt, b2, s0, s1, ph0, pl0, ph1, pl1, held):
+def old_kernel(n, blocks, sg, tg, moment, lse_out, lse_own, carried, xh, xl, rt, rc, lt, b2, s0, s1, ph0, pl0, ph1, pl1, held, padded):
     for t in range(blocks):
         hi, low = split(features(tg[t]))
         rt[0:FEAT, tile(t)] = hi
@@ -245,7 +245,10 @@
         xh[:, tile(t)] = hi
         xl[:, tile(t)] = low
         lt[BIAS:DEPTH, tile(t)] = extra({3: 1.0, 4: 1.0, 5: 1.0})
-    lh, ll = left_operand(xh[...], xl[...], moment[...])
+    used = slice(LATENT, LATENT + RANK)
+    padded[...] = jnp.zeros(padded.shape, f32)
+    padded[used, used] = moment[...]
+    lh, ll = left_operand(xh[...], xl[...], padded[...])
     lt[0:FEAT, :] = lh
     lt[FEAT : 2 * FEAT, :] = lh
     lt[2 * FEAT : BIAS, :] = ll
@@ -420,7 +423,6 @@
     tg = lax.all_gather(target, "src", axis=0)
     bs, bt = n_tgt, n_src
     rows, cols = bs * LANES, bt * LANES
-    old = jnp.pad(old_moment, ((LATENT, LANES - LATENT - RANK),) * 2)
 
     lse, own, carried, xh, xl, rt, rc = call(
         functools.partial(old_kernel, n_tgt, bs),
@@ -443,9 +445,10 @@
             ((cols, CHUNK), bf16),
             ((cols, CHUNK), bf16),
             ((1, rows), f32),
+            ((LANES, LANES), f32),
         ],
         name="old_plan",
-    )(sg, tg, old)
+    )(sg, tg, old_moment)
     f, moment = call(
         functools.partial(moment_kernel, n_tgt, bs),
         [((bs, LANES), f32), ((n_tgt, 16, LANES), f32)],

time: 139 us -> 139 us (level)
  no operation moved by 1% of the time
where the time goes in v7:
time: 139 us; the launch traced here: 137 us
  blocking collectives  105 us (76%)
  Pallas kernels  23.1 us (17%)
  starting transfers between devices  7.62 us (5%)
    all_to_all x7, blocking collectives, swap(): return lax.all_to_all(x, axis, 0, 0)  82.6 us
    pallas_call x9, Pallas kernels, call(): pl.pallas_call(kernel, out_shape=[jax.ShapeDtypeStruct(s, d) for s, d in...  23.1 us
    all_gather x1, blocking collectives, shards(): tg = lax.all_gather(target, 'src', axis=0)  22.5 us
    all_to_all x1, starting transfers between devices, swap(): return lax.all_to_all(x, axis, 0, 0)  7.62 us
  transfers between devices with their start and end apart: 1, of which 0 were waited for; matrix products, arithmetic and copies ran while one was open for 0% of the time, Pallas kernels for 0%

profile of v7, /device:TPU:2, one launch (start us, length us, event | category | flops | bytes accessed | tf_op | source)
XLA Modules:
  0.0 136.6 jit_solution(2690742574253752322)
XLA Ops:
  0.6 1.9 %pack.1 = (f32[16,112,128]{2,1,0:T(8,128)}, f32[112,128]{1,0:T(8,128)}) custom-call(f32[32,128]{1,0:T(8,128)} %bitcast.30, f32[34,128]{1,0:T(8,128)} %bitcast.26, f32[34,128]{1,0:T(8,128)} %bitcast.27, f32[1,128]{1,0:T(1,128)} %bitcast.32, f32[32,128]{1,0:T(8,128)} %bitcast.31, f32[34,1,128]{2,1,0:T(1,128)} %bitcast.28, f32[34,1,128]{2,1,0:T(1,128)} %bitcast.29, ...), custom_call_target="tpu_custom_call" | custom-call | tf_op jit(solution)/shard_map/pack/pallas_call | solution.py:391
  2.5 0.0 copy-start.1
  2.6 7.6 %all-to-all-start = ((f32[16,112,128]{2,1,0:T(8,128)}), f32[16,112,128]{2,1,0:T(8,128)S(1)}, u32[]{:S(2)}, u32[]{:S(2)}) async-start(f32[16,112,128]{2,1,0:T(8,128)} %get-tuple-element.25), calls=%async_computation | async-start | bytes 1835008 | tf_op jit(solution)/shard_map/all_to_all | solution.py:404
  10.2 0.0 copy-done.1
  10.2 0.0 copy-start
  10.2 22.5 %all-gather = f32[1792,128]{1,0:T(8,128)S(1)} all-gather(f32[112,128]{1,0:T(8,128)S(1)} %copy-done.1), channel_id=2, replica_groups=mesh['src'=16,'tgt'=16] {'src'}, dimensions={0}, use_global_device_ids=true | all-gather | bytes 974848 | tf_op jit(solution)/shard_map/all_gather | solution.py:423
  32.7 0.0 all-to-all-done.sg.gathered
  32.7 0.0 copy-done
  32.7 6.7 %old_plan.1 = (f32[16,16,128]{2,1,0:T(8,128)S(1)}, f32[16,128]{1,0:T(8,128)S(1)}, f32[48,2048]{1,0:T(8,128)S(1)}, bf16[80,2048]{1,0:T(8,128)(2,1)S(1)}, bf16[80,...) custom-call(f32[16,112,128]{2,1,0:T(8,128)S(1)} %all-to-all-done.sg.gathered, ...), custom_call_target="tpu_custom_call" | custom-call | tf_op jit(solution)/shard_map/old_plan/pallas_call | solution.py:391
  39.4 13.7 %all_to_all.40.parts = f32[16,16,128]{2,1,0:T(8,128)S(1)} all-to-all(f32[16,16,128]{2,1,0:T(8,128)S(1)} %get-tuple-element.27), channel_id=1, replica_groups=mesh['src'=16,'tgt'=16] {'tgt'}, dimensions={0} | all-to-all | bytes 262144 | tf_op jit(solution)/shard_map/all_to_all | solution.py:404
  53.1 0.4 moment.3
  53.5 11.1 %all_to_all.41.parts = f32[16,16,128]{2,1,0:T(8,128)S(1)} all-to-all(f32[16,16,128]{2,1,0:T(8,128)S(1)} %get-tuple-element.30), channel_id=1, replica_groups=mesh['src'=16,'tgt'=16] {'tgt'}, dimensions={0} | all-to-all | bytes 262144 | tf_op jit(solution)/shard_map/all_to_all | solution.py:404
  64.6 12.3 %all_to_all.42.parts = f32[16,16,128]{2,1,0:T(8,128)S(1)} all-to-all(f32[16,16,128]{2,1,0:T(8,128)S(1)} %moment_sum.1), channel_id=1, replica_groups=mesh['src'=16,'tgt'=16] {'src'}, dimensions={0} | all-to-all | bytes 262144 | tf_op jit(solution)/shard_map/all_to_all | solution.py:404
  76.9 4.5 %first_g.1 = (f32[16,16,128]{2,1,0:T(8,128)S(1)}, f32[16,128]{1,0:T(8,128)S(1)}, bf16[2048,256]{1,0:T(8,128)(2,1)S(1)}, bf16[256,2048]{1,0:T(8,128)(2,1)S(1)}) custom-call(f32[16,16,128]{2,1,0:T(8,128)S(1)} %all_to_all.42.parts, f32[16,128]{1,0:T(8,128)S(1)} %get-tuple-element.31.f, bf16[80,2048]{1,0:T(8,128)(2,1)S(1)} %get-tuple-element.32.xh, ...), custom_call_target="tpu_custom_call" | custom-call | tf_op jit(solution)/shard_map/first_g/pallas_call | solution.py:391
  81.4 11.6 %all_to_all.43.parts = f32[16,16,128]{2,1,0:T(8,128)S(1)} all-to-all(f32[16,16,128]{2,1,0:T(8,128)S(1)} %get-tuple-element.35), channel_id=1, replica_groups=mesh['src'=16,'tgt'=16] {'src'}, dimensions={0} | all-to-all | bytes 262144 | tf_op jit(solution)/shard_map/all_to_all | solution.py:404
  93.0 3.2 %first_f.1 = (f32[16,16,128]{2,1,0:T(8,128)S(1)}, bf16[256,2048]{1,0:T(8,128)(2,1)S(1)}, bf16[2048,256]{1,0:T(8,128)(2,1)S(1)}) custom-call(f32[16,16,128]{2,1,0:T(8,128)S(1)} %all_to_all.43.parts, f32[16,112,128]{2,1,0:T(8,128)S(1)} %bitcast.23, f32[16,128]{1,0:T(8,128)S(1)} %get-tuple-element.31.f, ...), custom_call_target="tpu_custom_call", output_to_operand_aliasing={{1}: (5, {}), {2}: (6, {})} | custom-call | tf_op jit(solution)/shard_map/first_f/pallas_call | solution.py:391
  96.1 11.3 %all_to_all.44.parts = f32[16,16,128]{2,1,0:T(8,128)S(1)} all-to-all(f32[16,16,128]{2,1,0:T(8,128)S(1)} %get-tuple-element.39), channel_id=1, replica_groups=mesh['src'=16,'tgt'=16] {'tgt'}, dimensions={0} | all-to-all | bytes 262144 | tf_op jit(solution)/shard_map/all_to_all | solution.py:404
  107.5 2.8 %second_g.1 = (f32[16,16,128]{2,1,0:T(8,128)S(1)}, bf16[256,2048]{1,0:T(8,128)(2,1)S(1)}) custom-call(f32[16,16,128]{2,1,0:T(8,128)S(1)} %all_to_all.44.parts, f32[16,112,128]{2,1,0:T(8,128)S(1)} %all-to-all-done.sg.gathered, f32[16,128]{1,0:T(8,128)S(1)} %get-tuple-element.36.last, ...), custom_call_target="tpu_custom_call", output_to_operand_aliasing={{1}: (4, {})} | custom-call | tf_op jit(solution)/shard_map/second_g/pallas_call | solution.py:391
  110.4 11.3 %all_to_all.45.parts = f32[16,16,128]{2,1,0:T(8,128)S(1)} all-to-all(f32[16,16,128]{2,1,0:T(8,128)S(1)} %get-tuple-element.42), channel_id=1, replica_groups=mesh['src'=16,'tgt'=16] {'src'}, dimensions={0} | all-to-all | bytes 262144 | tf_op jit(solution)/shard_map/all_to_all | solution.py:404
  121.7 2.9 %second_f.1 = (f32[16,16,128]{2,1,0:T(8,128)S(1)}, f32[16,128]{1,0:T(8,128)S(1)}, bf16[256,2048]{1,0:T(8,128)(2,1)S(1)}) custom-call(f32[16,16,128]{2,1,0:T(8,128)S(1)} %all_to_all.45.parts, f32[16,112,128]{2,1,0:T(8,128)S(1)} %bitcast.24, f32[16,128]{1,0:T(8,128)S(1)} %get-tuple-element.31.f, ...), custom_call_target="tpu_custom_call", output_to_operand_aliasing={{2}: (4, {})} | custom-call | tf_op jit(solution)/shard_map/second_f/pallas_call | solution.py:391
  124.5 11.3 %all_to_all.46.parts = f32[16,16,128]{2,1,0:T(8,128)S(1)} all-to-all(f32[16,16,128]{2,1,0:T(8,128)S(1)} %get-tuple-element.44), channel_id=1, replica_groups=mesh['src'=16,'tgt'=16] {'tgt'}, dimensions={0} | all-to-all | bytes 262144 | tf_op jit(solution)/shard_map/all_to_all | solution.py:404
  135.9 0.7 last.1
  (1 shorter events, 0.0 us)
Async XLA Ops:
  2.5 7.6 %copy-start.1 = (f32[112,128]{1,0:T(8,128)S(1)}, f32[112,128]{1,0:T(8,128)}, u32[]{:S(2)}) copy-start(f32[112,128]{1,0:T(8,128)} %get-tuple-element.26) | copy-start | bytes 172036
  2.6 30.1 %all-to-all-start = ((f32[16,112,128]{2,1,0:T(8,128)}), f32[16,112,128]{2,1,0:T(8,128)S(1)}, u32[]{:S(2)}, u32[]{:S(2)}) async-start(f32[16,112,128]{2,1,0:T(8,128)} %get-tuple-element.25), calls=%async_computation | async-start | bytes 1835008 | tf_op jit(solution)/shard_map/all_to_all | solution.py:404
  10.2 22.5 %copy-start = (f32[34,34]{1,0:T(8,128)S(1)}, f32[34,34]{1,0:T(8,128)}, u32[]{:S(2)}) copy-start(f32[34,34]{1,0:T(8,128)} %moment.2) | copy-start | bytes 13876

commit v8 on v7

--- a/solution.py
+++ b/solution.py
@@ -146,14 +146,22 @@
 
 def pipeline(stream, fixed, s0, s1, reduce, beside):
     s = (s0, s1)
-    steps = stream.shape[0] // CHUNK
-    s0[...] = dot(stream[0:CHUNK, :], fixed[...])
-    for b in range(steps):
-        if b + 1 < steps:
-            s[(b + 1) % 2][...] = dot(stream[(b + 1) * CHUNK : (b + 2) * CHUNK, :], fixed[...])
-        for k in range(CHUNK // LANES):
-            beside(b * (CHUNK // LANES) + k)
-            reduce(b * (CHUNK // LANES) + k, s[b % 2], k * LANES)
+    cells = stream.shape[0]
+    edges = [0] + list(range(LANES, cells, CHUNK)) + [cells]
+    spans = list(zip(edges[:-1], edges[1:]))
+
+    def multiply(b):
+        start, end = spans[b]
+        s[b % 2][0 : end - start, :] = dot(stream[start:end, :], fixed[...])
+
+    multiply(0)
+    for b, (start, end) in enumerate(spans):
+        if b + 1 < len(spans):
+            multiply(b + 1)
+        for row in range(0, end - start, LANES):
+            t = (start + row) // LANES
+            beside(t)
+            reduce(t, s[b % 2], row)
 
 
 def lse_rows(beside, stream, fixed, out_ref, own_ref, s0, s1, tops, totals):
@@ -309,10 +317,9 @@
     fill = jnp.zeros((LANES - RIGHT, ch.shape[1]), bf16)
     ch, cl = jnp.concatenate([ch, fill], axis=0), jnp.concatenate([cl, fill], axis=0)
     x = dot_nt(hi, ch) + dot_nt(low, ch) + dot_nt(hi, cl)
-    second, third = pltpu.roll(x[16:32], MOMENT, 1), pltpu.roll(x[32:40], 2 * MOMENT, 1)
-    packed = x[0:16] + second + jnp.concatenate([third, jnp.zeros_like(third)], axis=0)
+    packed = x[0:12] + pltpu.roll(x[12:24], MOMENT, 1) + pltpu.roll(x[24:36], 2 * MOMENT, 1)
     for k in range(n):
-        moment_out[k] = packed
+        moment_out[k, :, 0, :] = packed
 
 
 def sum_kernel(n, parts, out):
@@ -324,15 +331,15 @@
 def unpack_moment(packed):
     first = pltpu.roll(packed, LATENT, 1)
     second = pltpu.roll(packed, LANES + LATENT - MOMENT, 1)
-    third = pltpu.roll(packed[0:8], LANES + LATENT - 2 * MOMENT, 1)
-    x = jnp.concatenate([first, second, third], axis=0)
+    third = pltpu.roll(packed, LANES + LATENT - 2 * MOMENT, 1)
+    x = jnp.concatenate([first, second, third, jnp.zeros((MOMENT - 36, LANES), f32)], axis=0)
     rows, lanes = iota(x.shape, 0), iota(x.shape, 1)
     x = jnp.where((rows < RANK) & (lanes >= LATENT) & (lanes < LATENT + RANK), x, 0.0)
     return jnp.concatenate([jnp.zeros((LATENT, LANES), f32), x, jnp.zeros((LANES - LATENT - MOMENT, LANES), f32)], axis=0)
 
 
 def first_g_kernel(blocks, parts, f, xh, xl, rc, out, own, lc, lt, *scratch):
-    moment = unpack_moment(jnp.sum(parts[...], axis=0))
+    moment = unpack_moment(jnp.sum(parts[...], axis=0)[:, 0, :])
     lh, ll = left_operand(xh[...], xl[...], moment)
     lt[0:FEAT, :] = lh
     lt[FEAT : 2 * FEAT, :] = lh
@@ -451,10 +458,10 @@
     )(sg, tg, old_moment)
     f, moment = call(
         functools.partial(moment_kernel, n_tgt, bs),
-        [((bs, LANES), f32), ((n_tgt, 16, LANES), f32)],
+        [((bs, LANES), f32), ((n_tgt, 12, 1, LANES), f32)],
         name="moment",
     )(swap(lse, "tgt"), own, carried, sg)
-    (moment,) = call(functools.partial(sum_kernel, n_src), [((n_src, 16, LANES), f32)], name="moment_sum")(
+    (moment,) = call(functools.partial(sum_kernel, n_src), [((n_src, 12, 1, LANES), f32)], name="moment_sum")(
         swap(moment, "tgt")
     )
     pipe = lambda cells, b: [((CHUNK, cells), f32)] * 2 + [((b, LANES), f32)] * 2

time: 139 us -> 138 us (level)
  no operation moved by 1% of the time
where the time goes in v8:
time: 138 us; the launch traced here: 136 us
  blocking collectives  104 us (75%)
  Pallas kernels  23.2 us (17%)
  starting transfers between devices  7.62 us (6%)
    all_to_all x7, blocking collectives, swap(): return lax.all_to_all(x, axis, 0, 0)  81.8 us
    pallas_call x9, Pallas kernels, call(): pl.pallas_call(kernel, out_shape=[jax.ShapeDtypeStruct(s, d) for s, d in...  23.2 us
    all_gather x1, blocking collectives, shards(): tg = lax.all_gather(target, 'src', axis=0)  22.5 us
    all_to_all x1, starting transfers between devices, swap(): return lax.all_to_all(x, axis, 0, 0)  7.62 us
  transfers between devices with their start and end apart: 1, of which 0 were waited for; matrix products, arithmetic and copies ran while one was open for 0% of the time, Pallas kernels for 0%

profile of v8, /device:TPU:2, one launch (start us, length us, event | category | flops | bytes accessed | tf_op | source)
XLA Modules:
  0.0 135.8 jit_solution(682401812478117048)
XLA Ops:
  0.6 1.9 %pack.1 = (f32[16,112,128]{2,1,0:T(8,128)}, f32[112,128]{1,0:T(8,128)}) custom-call(f32[32,128]{1,0:T(8,128)} %bitcast.30, f32[34,128]{1,0:T(8,128)} %bitcast.26, f32[34,128]{1,0:T(8,128)} %bitcast.27, f32[1,128]{1,0:T(1,128)} %bitcast.32, f32[32,128]{1,0:T(8,128)} %bitcast.31, f32[34,1,128]{2,1,0:T(1,128)} %bitcast.28, f32[34,1,128]{2,1,0:T(1,128)} %bitcast.29, ...), custom_call_target="tpu_custom_call" | custom-call | tf_op jit(solution)/shard_map/pack/pallas_call | solution.py:398
  2.5 0.0 copy-start.1
  2.6 7.6 %all-to-all-start = ((f32[16,112,128]{2,1,0:T(8,128)}), f32[16,112,128]{2,1,0:T(8,128)S(1)}, u32[]{:S(2)}, u32[]{:S(2)}) async-start(f32[16,112,128]{2,1,0:T(8,128)} %get-tuple-element.25), calls=%async_computation | async-start | bytes 1835008 | tf_op jit(solution)/shard_map/all_to_all | solution.py:411
  10.2 0.0 copy-done.1
  10.2 0.0 copy-start
  10.2 22.5 %all-gather = f32[1792,128]{1,0:T(8,128)S(1)} all-gather(f32[112,128]{1,0:T(8,128)S(1)} %copy-done.1), channel_id=2, replica_groups=mesh['src'=16,'tgt'=16] {'src'}, dimensions={0}, use_global_device_ids=true | all-gather | bytes 974848 | tf_op jit(solution)/shard_map/all_gather | solution.py:430
  32.7 0.0 all-to-all-done.sg.gathered
  32.7 0.0 copy-done
  32.7 6.7 %old_plan.1 = (f32[16,16,128]{2,1,0:T(8,128)S(1)}, f32[16,128]{1,0:T(8,128)S(1)}, f32[48,2048]{1,0:T(8,128)S(1)}, bf16[80,2048]{1,0:T(8,128)(2,1)S(1)}, bf16[80,...) custom-call(f32[16,112,128]{2,1,0:T(8,128)S(1)} %all-to-all-done.sg.gathered, ...), custom_call_target="tpu_custom_call" | custom-call | tf_op jit(solution)/shard_map/old_plan/pallas_call | solution.py:398
  39.4 13.7 %all_to_all.40.parts = f32[16,16,128]{2,1,0:T(8,128)S(1)} all-to-all(f32[16,16,128]{2,1,0:T(8,128)S(1)} %get-tuple-element.27), channel_id=1, replica_groups=mesh['src'=16,'tgt'=16] {'tgt'}, dimensions={0} | all-to-all | bytes 262144 | tf_op jit(solution)/shard_map/all_to_all | solution.py:411
  53.1 0.5 moment.3
  53.6 10.9 %all_to_all.41.parts = f32[16,12,1,128]{3,2,1,0:T(1,128)S(1)} all-to-all(f32[16,12,1,128]{3,2,1,0:T(1,128)S(1)} %get-tuple-element.30), channel_id=1, replica_groups=mesh['src'=16,'tgt'=16] {'tgt'}, dimensions={0} | all-to-all | bytes 196608 | tf_op jit(solution)/shard_map/all_to_all | solution.py:411
  64.4 0.1 moment_sum.1
  64.5 11.8 %all_to_all.42.parts = f32[16,12,1,128]{3,2,1,0:T(1,128)S(1)} all-to-all(f32[16,12,1,128]{3,2,1,0:T(1,128)S(1)} %moment_sum.1), channel_id=1, replica_groups=mesh['src'=16,'tgt'=16] {'src'}, dimensions={0} | all-to-all | bytes 196608 | tf_op jit(solution)/shard_map/all_to_all | solution.py:411
  76.4 4.7 %first_g.1 = (f32[16,16,128]{2,1,0:T(8,128)S(1)}, f32[16,128]{1,0:T(8,128)S(1)}, bf16[2048,256]{1,0:T(8,128)(2,1)S(1)}, bf16[256,2048]{1,0:T(8,128)(2,1)S(1)}) custom-call(f32[16,12,1,128]{3,2,1,0:T(1,128)S(1)} %all_to_all.42.parts, f32[16,128]{1,0:T(8,128)S(1)} %get-tuple-element.31.f, bf16[80,2048]{1,0:T(8,128)(2,1)S(1)} %get-tuple-element.32.xh, ...), custom_call_target="tpu_custom_call" | custom-call | tf_op jit(solution)/shard_map/first_g/pallas_call | solution.py:398
  81.0 11.3 %all_to_all.43.parts = f32[16,16,128]{2,1,0:T(8,128)S(1)} all-to-all(f32[16,16,128]{2,1,0:T(8,128)S(1)} %get-tuple-element.35), channel_id=1, replica_groups=mesh['src'=16,'tgt'=16] {'src'}, dimensions={0} | all-to-all | bytes 262144 | tf_op jit(solution)/shard_map/all_to_all | solution.py:411
  92.3 3.1 %first_f.1 = (f32[16,16,128]{2,1,0:T(8,128)S(1)}, bf16[256,2048]{1,0:T(8,128)(2,1)S(1)}, bf16[2048,256]{1,0:T(8,128)(2,1)S(1)}) custom-call(f32[16,16,128]{2,1,0:T(8,128)S(1)} %all_to_all.43.parts, f32[16,112,128]{2,1,0:T(8,128)S(1)} %bitcast.23, f32[16,128]{1,0:T(8,128)S(1)} %get-tuple-element.31.f, ...), custom_call_target="tpu_custom_call", output_to_operand_aliasing={{1}: (5, {}), {2}: (6, {})} | custom-call | tf_op jit(solution)/shard_map/first_f/pallas_call | solution.py:398
  95.4 11.4 %all_to_all.44.parts = f32[16,16,128]{2,1,0:T(8,128)S(1)} all-to-all(f32[16,16,128]{2,1,0:T(8,128)S(1)} %get-tuple-element.39), channel_id=1, replica_groups=mesh['src'=16,'tgt'=16] {'tgt'}, dimensions={0} | all-to-all | bytes 262144 | tf_op jit(solution)/shard_map/all_to_all | solution.py:411
  106.8 2.8 %second_g.1 = (f32[16,16,128]{2,1,0:T(8,128)S(1)}, bf16[256,2048]{1,0:T(8,128)(2,1)S(1)}) custom-call(f32[16,16,128]{2,1,0:T(8,128)S(1)} %all_to_all.44.parts, f32[16,112,128]{2,1,0:T(8,128)S(1)} %all-to-all-done.sg.gathered, f32[16,128]{1,0:T(8,128)S(1)} %get-tuple-element.36.last, ...), custom_call_target="tpu_custom_call", output_to_operand_aliasing={{1}: (4, {})} | custom-call | tf_op jit(solution)/shard_map/second_g/pallas_call | solution.py:398
  109.6 11.3 %all_to_all.45.parts = f32[16,16,128]{2,1,0:T(8,128)S(1)} all-to-all(f32[16,16,128]{2,1,0:T(8,128)S(1)} %get-tuple-element.42), channel_id=1, replica_groups=mesh['src'=16,'tgt'=16] {'src'}, dimensions={0} | all-to-all | bytes 262144 | tf_op jit(solution)/shard_map/all_to_all | solution.py:411
  120.9 2.8 %second_f.1 = (f32[16,16,128]{2,1,0:T(8,128)S(1)}, f32[16,128]{1,0:T(8,128)S(1)}, bf16[256,2048]{1,0:T(8,128)(2,1)S(1)}) custom-call(f32[16,16,128]{2,1,0:T(8,128)S(1)} %all_to_all.45.parts, f32[16,112,128]{2,1,0:T(8,128)S(1)} %bitcast.24, f32[16,128]{1,0:T(8,128)S(1)} %get-tuple-element.31.f, ...), custom_call_target="tpu_custom_call", output_to_operand_aliasing={{2}: (4, {})} | custom-call | tf_op jit(solution)/shard_map/second_f/pallas_call | solution.py:398
  123.8 11.3 %all_to_all.46.parts = f32[16,16,128]{2,1,0:T(8,128)S(1)} all-to-all(f32[16,16,128]{2,1,0:T(8,128)S(1)} %get-tuple-element.44), channel_id=1, replica_groups=mesh['src'=16,'tgt'=16] {'tgt'}, dimensions={0} | all-to-all | bytes 262144 | tf_op jit(solution)/shard_map/all_to_all | solution.py:411
  135.1 0.7 last.1
Async XLA Ops:
  2.5 7.6 %copy-start.1 = (f32[112,128]{1,0:T(8,128)S(1)}, f32[112,128]{1,0:T(8,128)}, u32[]{:S(2)}) copy-start(f32[112,128]{1,0:T(8,128)} %get-tuple-element.26) | copy-start | bytes 172036
  2.6 30.1 %all-to-all-start = ((f32[16,112,128]{2,1,0:T(8,128)}), f32[16,112,128]{2,1,0:T(8,128)S(1)}, u32[]{:S(2)}, u32[]{:S(2)}) async-start(f32[16,112,128]{2,1,0:T(8,128)} %get-tuple-element.25), calls=%async_computation | async-start | bytes 1835008 | tf_op jit(solution)/shard_map/all_to_all | solution.py:411
  10.2 22.5 %copy-start = (f32[34,34]{1,0:T(8,128)S(1)}, f32[34,34]{1,0:T(8,128)}, u32[]{:S(2)}) copy-start(f32[34,34]{1,0:T(8,128)} %moment.2) | copy-start | bytes 13876

commit v9 on v8

--- a/solution.py
+++ b/solution.py
@@ -180,7 +180,7 @@
             ref[...] = x
         else:
             for k in range(ref.shape[0]):
-                ref[k] = x
+                ref[k, :, 0, :] = x
 
 
 def shifted_lse_rows(beside, stream, fixed, shift, s0, s1, tops, totals, *refs):
@@ -304,11 +304,11 @@
     lse = jnp.concatenate([held[:, tile(t)] for t in range(cells // LANES)], axis=0)
     lse_own[...] = lse
     for k in range(n):
-        lse_out[k] = lse
+        lse_out[k, :, 0, :] = lse
 
 
 def moment_kernel(n, blocks, parts, lse_own, carried, sg, f_out, moment_out):
-    f = LOG2E * pick(sg, ROW_LOGW, blocks) - combine(parts[...])
+    f = LOG2E * pick(sg, ROW_LOGW, blocks) - combine(parts[:, :, 0, :])
     f_out[...] = f
     weight = jnp.exp2(f + lse_own[...])
     left = [sg[t, ROW_RIGHT:PACK, :] * weight[t : t + 1] for t in range(blocks)]
@@ -357,7 +357,7 @@
 
 
 def updated(blocks, parts, gathered):
-    return LOG2E * pick(gathered, ROW_LOGW, blocks) - combine(parts[...])
+    return LOG2E * pick(gathered, ROW_LOGW, blocks) - combine(parts[:, :, 0, :])
 
 
 def potential(blocks, x, gathered):
@@ -434,7 +434,7 @@
     lse, own, carried, xh, xl, rt, rc = call(
         functools.partial(old_kernel, n_tgt, bs),
         [
-            ((n_tgt, bs, LANES), f32),
+            ((n_tgt, bs, 1, LANES), f32),
             ((bs, LANES), f32),
             ((RIGHT, rows), f32),
             ((FEAT, rows), bf16),
@@ -467,28 +467,28 @@
     pipe = lambda cells, b: [((CHUNK, cells), f32)] * 2 + [((b, LANES), f32)] * 2
     part, last_g, lc, lt = call(
         functools.partial(first_g_kernel, bs),
-        [((n_src, bt, LANES), f32), ((bt, LANES), f32), ((rows, DEPTH), bf16), ((DEPTH, rows), bf16)],
+        [((n_src, bt, 1, LANES), f32), ((bt, LANES), f32), ((rows, DEPTH), bf16), ((DEPTH, rows), bf16)],
         pipe(rows, bt),
         name="first_g",
     )(swap(moment, "src"), f, xh, xl, rc)
     fixed_t, fixed_s, stream_t = ((DEPTH, cols), bf16), ((DEPTH, rows), bf16), ((cols, DEPTH), bf16)
     part, rt, rc = call(
         functools.partial(first_f_kernel, bt),
-        [((n_tgt, bs, LANES), f32), fixed_t, stream_t],
+        [((n_tgt, bs, 1, LANES), f32), fixed_t, stream_t],
         pipe(cols, bs),
         name="first_f",
         aliases={5: 1, 6: 2},
     )(swap(part, "src"), tg, f, last_g, lc, rt, rc)
     part, _ = call(
         functools.partial(second_g_kernel, bs),
-        [((n_src, bt, LANES), f32), fixed_s],
+        [((n_src, bt, 1, LANES), f32), fixed_s],
         pipe(rows, bt),
         name="second_g",
         aliases={4: 1},
     )(swap(part, "tgt"), sg, last_g, rc, lt)
     part, x, _ = call(
         functools.partial(second_f_kernel, bt),
-        [((n_tgt, bs, LANES), f32), ((bt, LANES), f32), fixed_t],
+        [((n_tgt, bs, 1, LANES), f32), ((bt, LANES), f32), fixed_t],
         pipe(cols, bs),
         name="second_f",
         aliases={4: 2},

time: 138 us -> 140 us (1.014)
  Pallas kernels: 23.2 us -> 24.9 us
    pallas_call x9, Pallas kernels: 23.2 us -> 24.9 us  [call(): pl.pallas_call(kernel, out_shape=[jax.ShapeDtypeStruct(s, d) for s, d in...]
where the time goes in v9:
time: 140 us; the launch traced here: 138 us
  blocking collectives  104 us (74%)
  Pallas kernels  24.9 us (18%)
  starting transfers between devices  7.62 us (5%)
    all_to_all x7, blocking collectives, swap(): return lax.all_to_all(x, axis, 0, 0)  81.8 us
    pallas_call x9, Pallas kernels, call(): pl.pallas_call(kernel, out_shape=[jax.ShapeDtypeStruct(s, d) for s, d in...  24.9 us
    all_gather x1, blocking collectives, shards(): tg = lax.all_gather(target, 'src', axis=0)  22.5 us
    all_to_all x1, starting transfers between devices, swap(): return lax.all_to_all(x, axis, 0, 0)  7.62 us
  transfers between devices with their start and end apart: 1, of which 0 were waited for; matrix products, arithmetic and copies ran while one was open for 0% of the time, Pallas kernels for 0%

profile of v9, /device:TPU:2, one launch (start us, length us, event | category | flops | bytes accessed | tf_op | source)
XLA Modules:
  0.0 137.5 jit_solution(12504293982222043512)
XLA Ops:
  0.6 1.9 %pack.1 = (f32[16,112,128]{2,1,0:T(8,128)}, f32[112,128]{1,0:T(8,128)}) custom-call(f32[32,128]{1,0:T(8,128)} %bitcast.30, f32[34,128]{1,0:T(8,128)} %bitcast.26, f32[34,128]{1,0:T(8,128)} %bitcast.27, f32[1,128]{1,0:T(1,128)} %bitcast.32, f32[32,128]{1,0:T(8,128)} %bitcast.31, f32[34,1,128]{2,1,0:T(1,128)} %bitcast.28, f32[34,1,128]{2,1,0:T(1,128)} %bitcast.29, ...), custom_call_target="tpu_custom_call" | custom-call | tf_op jit(solution)/shard_map/pack/pallas_call | solution.py:398
  2.5 0.0 copy-start.1
  2.6 7.6 %all-to-all-start = ((f32[16,112,128]{2,1,0:T(8,128)}), f32[16,112,128]{2,1,0:T(8,128)S(1)}, u32[]{:S(2)}, u32[]{:S(2)}) async-start(f32[16,112,128]{2,1,0:T(8,128)} %get-tuple-element.25), calls=%async_computation | async-start | bytes 1835008 | tf_op jit(solution)/shard_map/all_to_all | solution.py:411
  10.2 0.0 copy-done.1
  10.2 0.0 copy-start
  10.2 22.5 %all-gather = f32[1792,128]{1,0:T(8,128)S(1)} all-gather(f32[112,128]{1,0:T(8,128)S(1)} %copy-done.1), channel_id=2, replica_groups=mesh['src'=16,'tgt'=16] {'src'}, dimensions={0}, use_global_device_ids=true | all-gather | bytes 974848 | tf_op jit(solution)/shard_map/all_gather | solution.py:430
  32.7 0.0 all-to-all-done.sg.gathered
  32.7 0.0 copy-done
  32.7 6.8 %old_plan.1 = (f32[16,16,1,128]{3,2,1,0:T(1,128)S(1)}, f32[16,128]{1,0:T(8,128)S(1)}, f32[48,2048]{1,0:T(8,128)S(1)}, bf16[80,2048]{1,0:T(8,128)(2,1)S(1)}, bf16...) custom-call(f32[16,112,128]{2,1,0:T(8,128)S(1)} %all-to-all-done.sg.gathered, ...), custom_call_target="tpu_custom_call" | custom-call | tf_op jit(solution)/shard_map/old_plan/pallas_call | solution.py:398
  39.5 13.7 %all_to_all.40.parts = f32[16,16,1,128]{3,2,1,0:T(1,128)S(1)} all-to-all(f32[16,16,1,128]{3,2,1,0:T(1,128)S(1)} %get-tuple-element.27), channel_id=1, replica_groups=mesh['src'=16,'tgt'=16] {'tgt'}, dimensions={0} | all-to-all | bytes 262144 | tf_op jit(solution)/shard_map/all_to_all | solution.py:411
  53.2 0.7 moment.3
  53.9 10.9 %all_to_all.41.parts = f32[16,12,1,128]{3,2,1,0:T(1,128)S(1)} all-to-all(f32[16,12,1,128]{3,2,1,0:T(1,128)S(1)} %get-tuple-element.30), channel_id=1, replica_groups=mesh['src'=16,'tgt'=16] {'tgt'}, dimensions={0} | all-to-all | bytes 196608 | tf_op jit(solution)/shard_map/all_to_all | solution.py:411
  64.8 0.1 moment_sum.1
  64.9 11.8 %all_to_all.42.parts = f32[16,12,1,128]{3,2,1,0:T(1,128)S(1)} all-to-all(f32[16,12,1,128]{3,2,1,0:T(1,128)S(1)} %moment_sum.1), channel_id=1, replica_groups=mesh['src'=16,'tgt'=16] {'src'}, dimensions={0} | all-to-all | bytes 196608 | tf_op jit(solution)/shard_map/all_to_all | solution.py:411
  76.7 4.7 %first_g.1 = (f32[16,16,1,128]{3,2,1,0:T(1,128)S(1)}, f32[16,128]{1,0:T(8,128)S(1)}, bf16[2048,256]{1,0:T(8,128)(2,1)S(1)}, bf16[256,2048]{1,0:T(8,128)(2,1)S(1)}) custom-call(f32[16,12,1,128]{3,2,1,0:T(1,128)S(1)} %all_to_all.42.parts, f32[16,128]{1,0:T(8,128)S(1)} %get-tuple-element.31.f, bf16[80,2048]{1,0:T(8,128)(2,1)S(1)} %get-tuple-element.32.xh, ...), custom_call_target="tpu_custom_call" | custom-call | tf_op jit(solution)/shard_map/first_g/pallas_call | solution.py:398
  81.4 11.3 %all_to_all.43.parts = f32[16,16,1,128]{3,2,1,0:T(1,128)S(1)} all-to-all(f32[16,16,1,128]{3,2,1,0:T(1,128)S(1)} %get-tuple-element.35), channel_id=1, replica_groups=mesh['src'=16,'tgt'=16] {'src'}, dimensions={0} | all-to-all | bytes 262144 | tf_op jit(solution)/shard_map/all_to_all | solution.py:411
  92.7 3.4 %first_f.1 = (f32[16,16,1,128]{3,2,1,0:T(1,128)S(1)}, bf16[256,2048]{1,0:T(8,128)(2,1)S(1)}, bf16[2048,256]{1,0:T(8,128)(2,1)S(1)}) custom-call(f32[16,16,1,128]{3,2,1,0:T(1,128)S(1)} %all_to_all.43.parts, f32[16,112,128]{2,1,0:T(8,128)S(1)} %bitcast.23, f32[16,128]{1,0:T(8,128)S(1)} %get-tuple-element.31.f, ...), custom_call_target="tpu_custom_call", output_to_operand_aliasing={{1}: (5, {}), {2}: (6, {})} | custom-call | tf_op jit(solution)/shard_map/first_f/pallas_call | solution.py:398
  96.1 11.4 %all_to_all.44.parts = f32[16,16,1,128]{3,2,1,0:T(1,128)S(1)} all-to-all(f32[16,16,1,128]{3,2,1,0:T(1,128)S(1)} %get-tuple-element.39), channel_id=1, replica_groups=mesh['src'=16,'tgt'=16] {'tgt'}, dimensions={0} | all-to-all | bytes 262144 | tf_op jit(solution)/shard_map/all_to_all | solution.py:411
  107.5 3.3 %second_g.1 = (f32[16,16,1,128]{3,2,1,0:T(1,128)S(1)}, bf16[256,2048]{1,0:T(8,128)(2,1)S(1)}) custom-call(f32[16,16,1,128]{3,2,1,0:T(1,128)S(1)} %all_to_all.44.parts, f32[16,112,128]{2,1,0:T(8,128)S(1)} %all-to-all-done.sg.gathered, f32[16,128]{1,0:T(8,128)S(1)} %get-tuple-element.36.last, ...), custom_call_target="tpu_custom_call", output_to_operand_aliasing={{1}: (4, {})} | custom-call | tf_op jit(solution)/shard_map/second_g/pallas_call | solution.py:398
  110.8 11.3 %all_to_all.45.parts = f32[16,16,1,128]{3,2,1,0:T(1,128)S(1)} all-to-all(f32[16,16,1,128]{3,2,1,0:T(1,128)S(1)} %get-tuple-element.42), channel_id=1, replica_groups=mesh['src'=16,'tgt'=16] {'src'}, dimensions={0} | all-to-all | bytes 262144 | tf_op jit(solution)/shard_map/all_to_all | solution.py:411
  122.1 3.1 %second_f.1 = (f32[16,16,1,128]{3,2,1,0:T(1,128)S(1)}, f32[16,128]{1,0:T(8,128)S(1)}, bf16[256,2048]{1,0:T(8,128)(2,1)S(1)}) custom-call(f32[16,16,1,128]{3,2,1,0:T(1,128)S(1)} %all_to_all.45.parts, f32[16,112,128]{2,1,0:T(8,128)S(1)} %bitcast.24, f32[16,128]{1,0:T(8,128)S(1)} %get-tuple-element.31.f, ...), custom_call_target="tpu_custom_call", output_to_operand_aliasing={{2}: (4, {})} | custom-call | tf_op jit(solution)/shard_map/second_f/pallas_call | solution.py:398
  125.3 11.3 %all_to_all.46.parts = f32[16,16,1,128]{3,2,1,0:T(1,128)S(1)} all-to-all(f32[16,16,1,128]{3,2,1,0:T(1,128)S(1)} %get-tuple-element.44), channel_id=1, replica_groups=mesh['src'=16,'tgt'=16] {'tgt'}, dimensions={0} | all-to-all | bytes 262144 | tf_op jit(solution)/shard_map/all_to_all | solution.py:411
  136.6 0.9 last.1
Async XLA Ops:
  2.5 7.6 %copy-start.1 = (f32[112,128]{1,0:T(8,128)S(1)}, f32[112,128]{1,0:T(8,128)}, u32[]{:S(2)}) copy-start(f32[112,128]{1,0:T(8,128)} %get-tuple-element.26) | copy-start | bytes 172036
  2.6 30.1 %all-to-all-start = ((f32[16,112,128]{2,1,0:T(8,128)}), f32[16,112,128]{2,1,0:T(8,128)S(1)}, u32[]{:S(2)}, u32[]{:S(2)}) async-start(f32[16,112,128]{2,1,0:T(8,128)} %get-tuple-element.25), calls=%async_computation | async-start | bytes 1835008 | tf_op jit(solution)/shard_map/all_to_all | solution.py:411
  10.2 22.5 %copy-start = (f32[34,34]{1,0:T(8,128)S(1)}, f32[34,34]{1,0:T(8,128)}, u32[]{:S(2)}) copy-start(f32[34,34]{1,0:T(8,128)} %moment.2) | copy-start | bytes 13876
